TPU v7x, 128 devices: a whole 4x4x4 slice. The times are simulated.
128 devices in a mesh: grp: 2 (over core), aux: 32 (over y, z_hi, x), tr: 2 (over z_lo).
Axes of the slice: x: 4, y: 4, z: 4 (z_hi: 2, z_lo: 2; z = z_hi * 2 + z_lo), core: 2. Of those that a mesh axis runs over, the one named last changes fastest.
Arguments:
- trial_vectors: float32 [64, 8, 512], P('aux', None, 'tr'), may hold values from -6 to 6
- energy_val: float32 [64], P('aux'), may hold values from -1 to -0.2
- energy_cond: float32 [512], P('tr'), may hold values from 0.2 to 2
- coef_occ: bfloat16 [2048, 64, 64], P('aux'), may hold values from -0.75 to 0.75
- coef_virt: bfloat16 [2048, 512, 512], P('aux', 'tr'), may hold values from -0.005859375 to 0.005859375
- pair_coef: bfloat16 [64, 512, 2048], P('aux', 'tr'), may hold values from -0.03125 to 0.03125
- live_aux: int32 [32], P('aux'), may hold values from 16 to 64, as said below
Outputs:
- applied: float32 [64, 8, 512], P('aux', None, 'tr')
- intersection: float32 [8, 8], replicated
Inputs may be any that keep to these rules, and one draw needn't show every extreme that they name: `live_aux`: equals 64 on at least one shard.
All inputs are finite; a program needn't handle non-finite values.
Results may differ from a plain program's by a relative error of at most 0.0048.
Values may be sent and summed in bfloat16 or wider, within the bound.
No kernel may reach another device: no remote copies, remote signals or barrier semaphores. Data moves between devices by JAX's collectives and lax.ppermute only.
A program may use at most 64 MiB of HBM per device.

v0:
```python
import math

import jax
import jax.numpy as jnp
from jax import lax
from jax.sharding import PartitionSpec as P

V = 64
C = 512


def apply_hamiltonian(vectors, energy_gap, coef_occ, coef_virt, pair_coef, live_aux):
    rounded = vectors.astype(jnp.bfloat16)
    gathered = lax.all_gather(rounded, "aux", axis=0, tiled=True)
    group_index = lax.axis_index("grp")
    slots = coef_occ.shape[0]
    live_count = live_aux[0]
    zero_slot = jnp.zeros((), jnp.int32)
    range_high = jnp.where(group_index == 0, live_count, zero_slot)
    block_size = math.gcd(slots, 8)
    first_block = zero_slot // block_size
    last_block = (range_high + block_size - 1) // block_size
    full_vectors = gathered.shape[1]
    full_cond = coef_virt.shape[2]

    def one_block(block_index, running):
        slot_start = block_index * block_size
        piece_occ = lax.dynamic_slice_in_dim(coef_occ, slot_start, block_size, 0)
        piece_virt = lax.dynamic_slice_in_dim(coef_virt, slot_start, block_size, 0)
        slot_ids = slot_start + lax.iota(jnp.int32, block_size)
        keep_mask = ((slot_ids >= zero_slot) & (slot_ids < range_high)).astype(jnp.float32)
        blended = jnp.einsum(
            "puv,vkc->pukc", piece_occ, gathered, preferred_element_type=jnp.float32
        )
        blended = (blended * keep_mask[:, None, None, None]).astype(jnp.bfloat16)
        return running + jnp.einsum(
            "pukc,pcd->ukd", blended, piece_virt, preferred_element_type=jnp.float32
        )

    zero_term = jnp.zeros(
        (lax.axis_size("aux") * vectors.shape[0], full_vectors, full_cond), jnp.float32
    )
    direct_term = lax.psum_scatter(
        lax.fori_loop(first_block, last_block, one_block, zero_term),
        "aux",
        scatter_dimension=0,
        tiled=True,
    )
    direct_term = lax.psum_scatter(direct_term, "tr", scatter_dimension=2, tiled=True)
    is_exchange = group_index == 1
    projection = lax.cond(
        is_exchange,
        lambda: jnp.einsum("vcp,vkc->kp", pair_coef, rounded, preferred_element_type=jnp.float32),
        lambda: jnp.zeros((vectors.shape[1], pair_coef.shape[2]), jnp.float32),
    )
    projection = lax.psum(projection, ("aux", "tr"))
    projection_b = projection.astype(jnp.bfloat16)
    exchange_term = lax.cond(
        is_exchange,
        lambda: jnp.einsum(
            "vcp,kp->vkc", pair_coef, projection_b, preferred_element_type=jnp.float32
        ),
        lambda: jnp.zeros(vectors.shape, jnp.float32),
    )
    combined = lax.psum(direct_term + exchange_term, "grp")
    return energy_gap[:, None, :] * vectors + combined


def body(trial_vectors, energy_val, energy_cond, coef_occ, coef_virt, pair_coef, live_aux):
    energy_gap = energy_cond[None, :] - energy_val[:, None]
    applied_first = apply_hamiltonian(
        trial_vectors, energy_gap, coef_occ, coef_virt, pair_coef, live_aux
    )
    partial_intersection = jnp.einsum(
        "vkc,vjc->kj", trial_vectors, applied_first, precision=lax.Precision.HIGHEST
    )
    intersection = lax.psum(partial_intersection, ("aux", "tr")) / (V * C)
    residual = applied_first - jnp.einsum(
        "vkc,kj->vjc", trial_vectors, intersection, precision=lax.Precision.HIGHEST
    )
    correction = residual / energy_gap[:, None, :]
    applied = apply_hamiltonian(correction, energy_gap, coef_occ, coef_virt, pair_coef, live_aux)
    return (applied, intersection)


def solution(mesh):
    in_specs = (
        P("aux", None, "tr"),
        P("aux"),
        P("tr"),
        P("aux", None, None),
        P("aux", "tr", None),
        P("aux", "tr", None),
        P("aux"),
    )
    out_specs = (P("aux", None, "tr"), P())
    return jax.shard_map(body, mesh=mesh, in_specs=in_specs, out_specs=out_specs, check_vma=False)
```

profile of v0, /device:TPU:1, one launch (start us, length us, event | category | flops | bytes accessed | tf_op | source)
XLA Modules:
  0.0 1505.6 jit_solution(12991591668244876826)
XLA Ops:
  7.2 0.0 reduce-scatter.5.cloned.1.call-start
  7.9 0.7 convert_element_type.40
  8.6 83.8 %all_gather.6 = bf16[64,8,256]{2,1,0:T(8,128)(2,1)S(1)} all-gather(bf16[2,8,256]{2,1,0:T(8,128)(2,1)S(1)} %convert_element_type.40), channel_id=1, replica_groups=mesh['grp'=2,'aux'=32,'tr'=2] {'aux'}, dimensions={0}, use_global_device_ids=true | all-gather | bytes 270336 | tf_op jit(solution)/shard_map/all_gather | solution.py:14
  92.4 0.1 broadcast.62.clone
  92.5 0.0 copy-start
  92.5 0.0 copy-start.2
  92.6 0.0 copy-start.4
  92.6 0.0 copy-start.5
  92.6 0.9 copy-done.2
  93.5 0.0 reduce-scatter.5.cloned.1.call-update
  93.5 0.0 reduce-scatter.7.cloned.1.call-start
  93.6 0.9 copy-done
  94.5 0.0 copy-start.3
  94.5 0.4 conditional.4
  94.5 0.4 convolution_bitcast_fusion
  94.9 0.0 copy-done.4
  94.9 0.0 copy-done.5
  94.9 0.1 broadcast_subtract_fusion
  95.0 203.2 %reduce-scatter.5.cloned.1.call-done = f32[2,8,512]{2,1,0:T(8,128)} async-done(((f32[64,8,512]{2,1,0:T(8,128)}), f32[2,8,512]{2,1,0:T(8,128)}) %reduce-scatter.5.cloned.1.call-update) | async-done | bytes 32784 | tf_op jit(solution)/shard_map/reduce_scatter | solution.py:43
  298.1 0.0 reduce-scatter.7.cloned.1.call-update
  298.1 0.0 reduce-scatter.9.cloned.1.call-start
  298.2 287.8 %psum.35 = bf16[8,2048]{1,0:T(8,128)(2,1)S(1)} all-reduce(f32[8,2048]{1,0:T(8,128)S(1)} %get-tuple-element.306), channel_id=1, replica_groups=mesh['grp'=2,'aux'=32,'tr'=2] {'aux','tr'}, use_global_device_ids=true, to_apply=%region_6.7 | all-reduce | flops 16384 | bytes 98304 | tf_op jit(solution)/shard_map/psum | solution.py:56
  586.0 0.6 conditional.5
  586.0 0.6 convolution_bitcast_fusion.1
  586.6 0.0 reduce-scatter.7.cloned.1.call-done
  586.6 0.7 add.77
  587.4 83.2 %psum.36 = f32[2,8,256]{2,1,0:T(8,128)S(1)} all-reduce(f32[2,8,256]{2,1,0:T(8,128)S(1)} %add.77), channel_id=1, replica_groups=mesh['grp'=2,'aux'=32,'tr'=2] {'grp'}, use_global_device_ids=true, to_apply=%region_9.10 | all-reduce | flops 4096 | bytes 32768 | tf_op jit(solution)/shard_map/psum | solution.py:65
  670.6 0.0 copy-done.3
  670.6 0.1 convolution_bitcast_fusion.5
  670.7 144.3 %psum.37 = f32[8,8]{0,1:T(8,128)S(1)} all-reduce(f32[8,8]{0,1:T(8,128)S(1)} %convolution_bitcast_fusion.5), channel_id=1, replica_groups=mesh['grp'=2,'aux'=32,'tr'=2] {'aux','tr'}, use_global_device_ids=true, to_apply=%region_10.11 | all-reduce | flops 64 | bytes 512 | tf_op jit(solution)/shard_map/psum | solution.py:77
  815.0 0.1 fusion.52
  815.1 75.2 %all_gather.7 = bf16[64,8,256]{2,1,0:T(8,128)(2,1)S(1)} all-gather(bf16[2,8,256]{2,1,0:T(8,128)(2,1)S(1)} %get-tuple-element.150), channel_id=1, replica_groups=mesh['grp'=2,'aux'=32,'tr'=2] {'aux'}, dimensions={0}, use_global_device_ids=true | all-gather | bytes 270336 | tf_op jit(solution)/shard_map/all_gather | solution.py:14
  890.4 0.1 broadcast.62
  890.5 0.0 copy-start.1
  890.5 1.0 copy-done.1
  891.5 0.0 reduce-scatter.9.cloned.1.call-update
  891.5 0.0 reduce-scatter.11.cloned.1.call-start
  891.6 0.4 conditional.6
  891.6 0.4 convolution_bitcast_fusion.2
  892.0 233.9 %reduce-scatter.9.cloned.1.call-done = f32[2,8,512]{2,1,0:T(8,128)} async-done(((f32[64,8,512]{2,1,0:T(8,128)}), f32[2,8,512]{2,1,0:T(8,128)}) %reduce-scatter.9.cloned.1.call-update) | async-done | bytes 32784 | tf_op jit(solution)/shard_map/reduce_scatter | solution.py:43
  1125.9 0.0 reduce-scatter.11.cloned.1.call-update
  1125.9 287.5 %psum.38 = bf16[8,2048]{1,0:T(8,128)(2,1)S(1)} all-reduce(f32[8,2048]{1,0:T(8,128)S(1)} %get-tuple-element.308), channel_id=1, replica_groups=mesh['grp'=2,'aux'=32,'tr'=2] {'aux','tr'}, use_global_device_ids=true, to_apply=%region_17.18 | all-reduce | flops 16384 | bytes 98304 | tf_op jit(solution)/shard_map/psum | solution.py:56
  1413.4 0.7 copy.10
  1414.1 0.6 conditional.7
  1414.1 0.6 convolution_bitcast_fusion.3
  1414.7 0.0 reduce-scatter.11.cloned.1.call-done
  1414.7 0.7 add.79
  1415.5 83.0 %psum.39 = f32[2,8,256]{2,1,0:T(8,128)S(1)} all-reduce(f32[2,8,256]{2,1,0:T(8,128)S(1)} %add.79), channel_id=1, replica_groups=mesh['grp'=2,'aux'=32,'tr'=2] {'grp'}, use_global_device_ids=true, to_apply=%region_20.21 | all-reduce | flops 4096 | bytes 32768 | tf_op jit(solution)/shard_map/psum | solution.py:65
  1498.5 0.6 multiply_add_fusion
  (3 shorter events, 0.0 us)
Async XLA Ops:
  7.2 290.9 %reduce-scatter.5.cloned.1.call-start = ((), (), s32[]{:S(2)}) async-start(), calls=%async_computation.4 | async-start | bytes 1081344 | tf_op jit(solution)/shard_map/reduce_scatter | solution.py:43
  92.5 2.0 copy-start
  92.5 1.0 copy-start.2
  92.6 2.3 copy-start.4
  92.6 2.3 copy-start.5
  93.5 493.1 %reduce-scatter.7.cloned.1.call-start = ((), (), s32[]{:S(2)}) async-start(), calls=%async_computation.5 | async-start | bytes 49152 | tf_op jit(solution)/shard_map/reduce_scatter | solution.py:49
  94.5 576.1 %copy-start.3 = (f32[2,8,256]{2,1,0:T(8,128)S(1)}, f32[2,8,256]{2,1,0:T(8,128)}, u32[]{:S(2)}) copy-start(f32[2,8,256]{2,1,0:T(8,128)} %param.19) | copy-start | bytes 49156
  298.1 827.8 %reduce-scatter.9.cloned.1.call-start = ((), (), s32[]{:S(2)}) async-start(), calls=%async_computation.6 | async-start | bytes 1081344 | tf_op jit(solution)/shard_map/reduce_scatter | solution.py:43
  890.5 1.0 copy-start.1
  891.5 523.2 %reduce-scatter.11.cloned.1.call-start = ((), (), s32[]{:S(2)}) async-start(), calls=%async_computation.7 | async-start | bytes 49152 | tf_op jit(solution)/shard_map/reduce_scatter | solution.py:49
Sparse Core Ops, SparseCore 0:
  93.7 204.3 reduce-scatter.4
  300.5 31.9 reduce-scatter.6
  891.6 234.2 reduce-scatter.8
  1128.1 31.4 reduce-scatter.10
where the time goes:
time: 1510 us
  blocking collectives  1040 us (69%)
  waiting for transfers between devices  437 us (29%)
    psum x2, blocking collectives, apply_hamiltonian(): projection = lax.psum(projection, ('aux', 'tr'))  575 us
    reduce_scatter x2, waiting for transfers between devices, apply_hamiltonian(): lax.psum_scatter(lax.fori_loop(first_block, last_block, one_block, zero_t...  437 us
    psum x2, blocking collectives, apply_hamiltonian(): combined = lax.psum(direct_term + exchange_term, 'grp')  166 us
    all_gather x2, blocking collectives, apply_hamiltonian(): gathered = lax.all_gather(rounded, 'aux', axis=0, tiled=True)  159 us
    psum x1, blocking collectives, body(): intersection = lax.psum(partial_intersection, ('aux', 'tr')) / (V * C)  144 us
  transfers between devices with their start and end apart: 4, of which 2 were waited for; matrix products, arithmetic and copies ran while one was open for 0% of the time, Pallas kernels for 0%

commit v1 on v0

v1 whole, which is shorter than its diff:
```python
import functools

import jax
import jax.numpy as jnp
from jax import lax
from jax.experimental import pallas as pl
from jax.experimental.pallas import tpu as pltpu
from jax.sharding import PartitionSpec as P

V = 64
C = 512
K = 8
HALF = 4
AUX = 32
TR = 2
CB = C // TR
PAIRS = AUX * TR
SLOTS = 64
NAUX = 2048
BLOCK = 8
TILES = NAUX // 128
F32 = jnp.float32
BF16 = jnp.bfloat16
VMEM = pl.BlockSpec(memory_space=pltpu.VMEM)
SMEM = pl.BlockSpec(memory_space=pltpu.SMEM)
NT = (((1,), (1,)), ((), ()))


def params(mib):
    return pltpu.CompilerParams(vmem_limit_bytes=mib * 2**20)


def dot(a, b):
    return jnp.dot(a, b, preferred_element_type=F32)


def lane_ids(shape):
    return lax.broadcasted_iota(jnp.int32, shape, len(shape) - 1)


def own_rows(core, rows):
    return jnp.where(core == 0, rows[:HALF], rows[HALF:])


def first_kernel(trial_ref, pair_ref, out_ref):
    rounded = [trial_ref[v].astype(BF16) for v in range(2)]
    wide = jnp.concatenate(rounded, axis=1)
    projection = dot(wide, pair_ref[...]).astype(BF16)
    for device in range(PAIRS):
        tile = device // 4
        out_ref[device, :, : 2 * CB] = wide
        out_ref[device, :, 2 * CB :] = projection[:, 128 * tile : 128 * tile + 128]


def direct_kernel(first, *refs):
    if first:
        (
            where_ref, live_ref, arrived_ref, occ_ref, virt_ref, trial_ref, gap_ref,
            out_ref, rows_ref, vectors_ref, blended_ref, total_ref,
        ) = refs
    else:
        (
            where_ref, live_ref, arrived_ref, occ_ref, virt_ref,
            out_ref, rows_ref, vectors_ref, blended_ref, total_ref,
        ) = refs
    step = pl.program_id(0)
    core, aux, tr = where_ref[0], where_ref[1], where_ref[2]

    @pl.when(step == 0)
    def _():
        total_ref[...] = jnp.zeros_like(total_ref)
        if first:
            for a in range(AUX):
                for t in range(TR):
                    slab = arrived_ref[2 * a + t].astype(F32)
                    for u in range(2):
                        for q in range(2):
                            at = CB * u + 128 * q
                            rows_ref[t, q, 16 * a + 8 * u : 16 * a + 8 * u + 8, :] = slab[:, at : at + 128]
            for k in range(HALF):
                for q in range(2):
                    part = rows_ref[tr, q, pl.ds(HALF * core + k, V, stride=K), :]
                    vectors_ref[k, :, 128 * q : 128 * q + 128] = part.astype(BF16)
        else:
            for a in range(AUX):
                for q in range(2):
                    part = arrived_ref[a, :, 128 * q : 128 * q + 128]
                    rows_ref[0, q, 8 * a : 8 * a + 8, :] = part.astype(F32)
            for k in range(HALF):
                for q in range(2):
                    part = rows_ref[0, q, pl.ds(k, V, stride=HALF), :]
                    vectors_ref[k, :, 128 * q : 128 * q + 128] = part.astype(BF16)

    occ = occ_ref[...].reshape(BLOCK * V, V)
    live = live_ref[0] - step * BLOCK
    slot = lax.broadcasted_iota(jnp.int32, (BLOCK * V, 1), 0) // V
    keep = (slot < live).astype(F32)
    for k in range(HALF):
        piece = (dot(occ, vectors_ref[k]) * keep).astype(BF16)
        for p in range(BLOCK):
            blended_ref[V * k : V * k + V, CB * p : CB * p + CB] = piece[V * p : V * p + V]
    product = dot(blended_ref[...], virt_ref[...])
    for q in range(C // 128):
        total_ref[q] += product[:, 128 * q : 128 * q + 128]

    @pl.when(step == SLOTS // BLOCK - 1)
    def _():
        if first:
            shares = jnp.zeros((K, HALF * V), F32)
            for t in range(TR):
                product = lax.dot_general(
                    jnp.concatenate([rows_ref[t, q] for q in range(2)], axis=1).astype(BF16),
                    jnp.concatenate([total_ref[2 * t + q] for q in range(2)], axis=1).astype(BF16),
                    NT,
                    preferred_element_type=F32,
                ).reshape(V, K, HALF * V)
                mine = lax.broadcasted_iota(jnp.int32, product.shape, 0)
                theirs = lane_ids(product.shape) % V
                shares += jnp.where(mine == theirs, product, 0.0).sum(axis=0)
            group = lane_ids(shares.shape) // V
            lanes = lane_ids((K, 128))
            kept = jnp.zeros((K, 128), F32)
            for j in range(HALF):
                column = jnp.where(group == j, shares, 0.0).sum(axis=1, keepdims=True)
                for v in range(2):
                    vectors = trial_ref[v]
                    other = own_rows(core, vectors)[j : j + 1] * gap_ref[v : v + 1]
                    column += (vectors * other).sum(axis=1, keepdims=True)
                high = column.astype(BF16).astype(F32)
                kept = jnp.where(lanes % 32 == j, high, kept)
                kept = jnp.where(lanes % 32 == HALF + j, column - high, kept)
            projection = jnp.zeros((K, 128), F32)
            for device in range(PAIRS):
                projection += arrived_ref[device, :, 2 * CB :].astype(F32)
            quarter = (TR * aux + tr) % 4
            extra = jnp.where(lanes // 32 == quarter, projection, kept)
        else:
            extra = jnp.zeros((K, 128), F32)
            for a in range(AUX):
                extra += arrived_ref[a, :, CB:].astype(F32)
        extra = extra.astype(BF16)
        for a in range(AUX):
            for t in range(TR):
                for q in range(2):
                    part = [
                        total_ref[2 * t + q, pl.ds(2 * a + u, HALF, stride=V), :]
                        for u in range(2)
                    ]
                    part = jnp.concatenate(part, axis=0).astype(BF16)
                    out_ref[2 * a + t, :, 128 * q : 128 * q + 128] = part
                out_ref[2 * a + t, :, CB:] = extra


def both_valence(rows):
    wide = (HALF, rows.shape[1])
    return jnp.concatenate(
        [jnp.broadcast_to(rows[v : v + 1], wide) for v in range(2)], axis=0
    )


def direct_sum(arrived_ref):
    total = jnp.zeros((2 * HALF, CB), F32)
    for device in range(PAIRS):
        total += arrived_ref[device, :, :CB].astype(F32)
    return total


def middle_kernel(
    where_ref, arrived_ref, pair_ref, trial_ref, gap_ref, out_ref, correction_ref, meet_ref
):
    core = where_ref[0]
    direct = direct_sum(arrived_ref)
    lanes = lane_ids((K, 128))
    tiles = []
    sums = [jnp.zeros((K, 128), F32) for _ in range(4)]
    for tile in range(TILES):
        whole = jnp.zeros((K, 128), F32)
        for quarter in range(4):
            extra = arrived_ref[4 * tile + quarter, :, CB:].astype(F32)
            whole = jnp.where(lanes // 32 == quarter, extra, whole)
            sums[quarter] += extra
        tiles.append(whole.astype(BF16))
    projection = jnp.concatenate(tiles, axis=1)
    exchange_full = lax.dot_general(projection, pair_ref[...], NT, preferred_element_type=F32)
    mine = own_rows(core, exchange_full)
    exchange = jnp.concatenate([mine[:, :CB], mine[:, CB:]], axis=0)
    shares = jnp.zeros((K, 128), F32)
    for quarter in range(4):
        shares += jnp.where(lanes // 32 == (quarter + 1) % 4, sums[quarter], 0.0)
    meet_exchange = lax.dot_general(projection, projection, NT, preferred_element_type=F32)
    meet = []
    for j in range(HALF):
        column = jnp.where(lanes % 32 % HALF == j, jnp.where(lanes % 32 < K, shares, 0.0), 0.0)
        column = column.sum(axis=1, keepdims=True)
        own = jnp.where(core == 0, meet_exchange[:, j : j + 1], meet_exchange[:, HALF + j : HALF + j + 1])
        meet.append((column + own) / (V * C))
    kept = jnp.zeros((K, 128), F32)
    for j in range(HALF):
        kept = jnp.where(lanes == j, meet[j], kept)
    meet_ref[...] = kept
    gap = both_valence(gap_ref[...])
    vectors = [trial_ref[v] for v in range(2)]
    trial = jnp.concatenate([own_rows(core, vectors[v]) for v in range(2)], axis=0)
    applied = gap * trial + direct + exchange
    overlap = jnp.concatenate(
        [(vectors[v] * meet[j]).sum(axis=0, keepdims=True) for v in range(2) for j in range(HALF)],
        axis=0,
    )
    correction = (applied - overlap) / gap
    correction_ref[...] = correction
    rounded = correction.astype(BF16)
    wide = jnp.concatenate([correction[:HALF], correction[HALF:]], axis=1)
    wide = jnp.concatenate([wide, jnp.zeros_like(wide)], axis=0).astype(BF16)
    projection = dot(wide, pair_ref[...]).astype(BF16)
    for a in range(AUX):
        tile = a // 2
        out_ref[a, :, :CB] = rounded
        out_ref[a, :, CB:] = projection[:, 128 * tile : 128 * tile + 128]


def last_kernel(arrived_ref, pair_ref, correction_ref, gap_ref, out_ref):
    direct = direct_sum(arrived_ref)
    tiles = []
    for tile in range(TILES):
        whole = arrived_ref[4 * tile, :, CB:].astype(F32) + arrived_ref[4 * tile + 1, :, CB:].astype(F32)
        tiles.append(whole.astype(BF16))
    projection = jnp.concatenate(tiles, axis=1)
    exchange = lax.dot_general(projection, pair_ref[...], NT, preferred_element_type=F32)
    exchange = jnp.concatenate([exchange[:HALF, :CB], exchange[:HALF, CB:]], axis=0)
    out_ref[...] = both_valence(gap_ref[...]) * correction_ref[...] + direct + exchange


def direct_call(first, where, live, arrived, occ, virt, *local):
    whole = [VMEM] * len(local)
    rows = (TR, 2, V * K, 128) if first else (1, 2, V * HALF, 128)
    return pl.pallas_call(
        functools.partial(direct_kernel, first),
        grid=(SLOTS // BLOCK,),
        in_specs=[
            SMEM,
            SMEM,
            VMEM,
            pl.BlockSpec((BLOCK, V, V), lambda i: (i, 0, 0)),
            pl.BlockSpec((BLOCK * CB, C), lambda i: (i, 0)),
            *whole,
        ],
        out_specs=VMEM,
        out_shape=jax.ShapeDtypeStruct((PAIRS, 2 * HALF, CB + 128), BF16),
        scratch_shapes=[
            pltpu.VMEM(rows, F32),
            pltpu.VMEM((HALF, V, CB), BF16),
            pltpu.VMEM((HALF * V, BLOCK * CB), BF16),
            pltpu.VMEM((C // 128, HALF * V, 128), F32),
        ],
        compiler_params=params(32),
    )(where, live, arrived, occ, virt, *local)


def body(trial_vectors, energy_val, energy_cond, coef_occ, coef_virt, pair_coef, live_aux):
    where = jnp.stack([lax.axis_index("grp"), lax.axis_index("aux"), lax.axis_index("tr")])
    where = where.astype(jnp.int32)
    gap = energy_cond[None, :] - energy_val[:, None]
    pair = pair_coef.reshape(2 * CB, NAUX)
    virt = coef_virt.reshape(SLOTS * CB, C)

    def exchange(x, axes):
        return lax.all_to_all(x, axes, split_axis=0, concat_axis=0, tiled=True)

    sent = pl.pallas_call(
        first_kernel,
        in_specs=[VMEM, VMEM],
        out_specs=VMEM,
        out_shape=jax.ShapeDtypeStruct((PAIRS, K, 2 * CB + 128), BF16),
        compiler_params=params(16),
    )(trial_vectors, pair)
    arrived = exchange(sent, ("aux", "tr"))
    sent = direct_call(True, where, live_aux, arrived, coef_occ, virt, trial_vectors, gap)
    arrived = exchange(sent, ("aux", "tr"))
    sent, correction, meet = pl.pallas_call(
        middle_kernel,
        in_specs=[SMEM] + [VMEM] * 4,
        out_specs=[VMEM] * 3,
        out_shape=[
            jax.ShapeDtypeStruct((AUX, 2 * HALF, CB + 128), BF16),
            jax.ShapeDtypeStruct((2 * HALF, CB), F32),
            jax.ShapeDtypeStruct((K, 128), F32),
        ],
        compiler_params=params(16),
    )(where, arrived, pair, trial_vectors, gap)
    arrived = exchange(sent, ("aux",))
    sent = direct_call(False, where, live_aux, arrived, coef_occ, virt)
    arrived = exchange(sent, ("aux", "tr"))
    applied = pl.pallas_call(
        last_kernel,
        in_specs=[VMEM] * 4,
        out_specs=VMEM,
        out_shape=jax.ShapeDtypeStruct((2 * HALF, CB), F32),
        compiler_params=params(16),
    )(arrived, pair, correction, gap)
    both = lax.all_gather(jnp.concatenate([applied, meet], axis=1), "grp")
    applied = both[:, :, :CB].reshape(2, 2, HALF, CB).transpose(1, 0, 2, 3).reshape(2, K, CB)
    intersection = jnp.concatenate([both[0, :, CB : CB + HALF], both[1, :, CB : CB + HALF]], axis=1)
    return (applied, intersection)


def solution(mesh):
    in_specs = (
        P("aux", None, "tr"),
        P("aux"),
        P("tr"),
        P("aux", None, None),
        P("aux", "tr", None),
        P("aux", "tr", None),
        P("aux"),
    )
    out_specs = (P("aux", None, "tr"), P())
    return jax.shard_map(body, mesh=mesh, in_specs=in_specs, out_specs=out_specs, check_vma=False)
```

time: 1510 us -> 115 us (0.08)
  blocking collectives: 1040 us -> 49.1 us
  waiting for transfers between devices: 437 us -> 11.9 us
  Pallas kernels: 0 us -> 21.2 us
    psum x5 -> x0, blocking collectives: 886 us -> none  [the longest x2 575 us: apply_hamiltonian(): projection = lax.psum(projection, ('aux', 'tr'))]
    reduce_scatter x4 -> x0, waiting for transfers between devices: 437 us -> none  [the longest x2 437 us: apply_hamiltonian(): lax.psum_scatter(lax.fori_loop(first_block, last_block, one_block, zero_t...]
    all_gather x2 -> x1, blocking collectives: 159 us -> 7.65 us  [body(): both = lax.all_gather(jnp.concatenate([applied, meet], axis=1), 'grp')]
    all_to_all x0 -> x3, blocking collectives: none -> 41.5 us  [exchange(): return lax.all_to_all(x, axes, split_axis=0, concat_axis=0, tiled=True)]
    pallas_call x0 -> x5, Pallas kernels: none -> 21.2 us  [the longest x2 18.4 us: direct_call(): pl.pallas_call(functools.partial(direct_kernel, first), grid=(SLOTS // BL...]
  transfers between devices with their start and end apart: 4 -> 1, of which waited for: 2 -> 1; matrix products, arithmetic and copies ran while one was open for 0% -> 1% of each run, Pallas kernels for 0% -> 0%
where the time goes in v1:
time: 115 us
  blocking collectives  49.1 us (43%)
  Pallas kernels  21.2 us (18%)
  local copies, waits for them, and re-layouts  18.1 us (16%)
  starting transfers between devices  12.2 us (11%)
  waiting for transfers between devices  11.9 us (10%)
  between operations  1.33 us (1%)
    all_to_all x3, blocking collectives, exchange(): return lax.all_to_all(x, axes, split_axis=0, concat_axis=0, tiled=True)  41.5 us
    pallas_call x2, Pallas kernels, direct_call(): pl.pallas_call(functools.partial(direct_kernel, first), grid=(SLOTS // BL...  18.4 us
    unnamed x21, local copies, waits for them, and re-layouts  17.5 us
    all_to_all x1, starting transfers between devices, exchange(): return lax.all_to_all(x, axes, split_axis=0, concat_axis=0, tiled=True)  12.2 us
    all_to_all x1, waiting for transfers between devices, exchange(): return lax.all_to_all(x, axes, split_axis=0, concat_axis=0, tiled=True)  11.9 us
    all_gather x1, blocking collectives, body(): both = lax.all_gather(jnp.concatenate([applied, meet], axis=1), 'grp')  7.65 us
  transfers between devices with their start and end apart: 1, of which 1 were waited for; matrix products, arithmetic and copies ran while one was open for 1% of the time, Pallas kernels for 0%

profile of v1, /device:TPU:1, one launch (start us, length us, event | category | flops | bytes accessed | tf_op | source)
XLA Modules:
  0.0 114.7 jit_solution(6405522600820003080)
XLA Ops:
  0.6 0.0 copy-start.2
  0.6 1.6 %copy-done.2 = bf16[2,256,2048]{2,1,0:T(8,128)(2,1)S(1)} copy-done((bf16[2,256,2048]{2,1,0:T(8,128)(2,1)S(1)}, bf16[2,256,2048]{2,1,0:T(8,128)(2,1)}, u32[]{:S(2)}) %copy-start.2) | copy-done | bytes 2097176
  2.2 0.0 copy-start.7
  2.2 0.7 copy-done.7
  2.9 0.0 copy-start.3
  2.9 0.0 copy-start.5
  2.9 0.4 shard_map.86
  3.3 0.0 copy-start.6
  3.3 0.9 copy-done.6
  4.2 12.2 %all-to-all-start = ((bf16[64,8,640]{2,1,0:T(8,128)(2,1)}), bf16[64,8,640]{2,1,0:T(8,128)(2,1)}, u32[]{:S(2)}, u32[]{:S(2)}) async-start(bf16[64,8,640]{2,1,0:T(8,128)(2,1)} %copy-done.6), calls=%async_computation | async-start | bytes 1310720 | tf_op jit(solution)/shard_map/all_to_all | solution.py:267
  17.1 0.1 pad_add_fusion.refs_0_.where_ref
  17.1 0.8 broadcast_subtract_fusion.refs_6_.gap_ref
  17.9 11.9 %all-to-all-done.refs_2_ = bf16[64,8,640]{2,1,0:T(8,128)(2,1)} async-done(((bf16[64,8,640]{2,1,0:T(8,128)(2,1)}), bf16[64,8,640]{2,1,0:T(8,128)(2,1)}, u32[]{:S(2)}, u32[]{:S(2)}) %all-to-all-start) | async-done | bytes 655392 | tf_op jit(solution)/shard_map/all_to_all | solution.py:267
  29.8 0.0 copy-start
  29.8 5.8 %copy-done = bf16[64,256,512]{2,1,0:T(8,128)(2,1)S(1)} copy-done((bf16[64,256,512]{2,1,0:T(8,128)(2,1)S(1)}, bf16[64,256,512]{2,1,0:T(8,128)(2,1)}, u32[]{:S(2)}) %copy-start) | copy-done | bytes 16777240
  35.6 0.0 copy-start.4
  35.6 1.2 %copy-done.4 = bf16[64,64,64]{2,1,0:T(8,128)(2,1)S(1)} copy-done((bf16[64,64,64]{2,1,0:T(8,128)(2,1)S(1)}, bf16[64,64,64]{2,1,0:T(8,128)(2,1)}, u32[]{:S(2)}) %copy-start.4) | copy-done | bytes 524312
  36.8 0.0 copy-start.8
  36.8 0.7 copy-done.8
  37.5 9.7 %shard_map.87 = bf16[64,8,384]{2,1,0:T(8,128)(2,1)S(1)} custom-call(s32[3]{0:T(128)S(1)} %pad_add_fusion.refs_0_.where_ref, s32[1]{0:T(128)S(6)} %copy.17.refs_1_, bf16[64,8,640]{2,1,0:T(8,128)(2,1)} %all-to-all-done.refs_2_, bf16[64,64,64]{2,1,0:T(8,128)(2,1)S(1)} %copy-done.4, bf16[16384,512]{1,0:T(8,128)(2,1)S(1)} %bitcast.11, ...), custom_call_target="tpu_custom_call" | custom-call | tf_op jit(solution)/shard_map/pallas_call | solution.py:236
  47.2 14.3 %all_to_all.20.arrived_ref = bf16[64,8,384]{2,1,0:T(8,128)(2,1)S(1)} all-to-all(bf16[64,8,384]{2,1,0:T(8,128)(2,1)S(1)} %shard_map.87), channel_id=1, replica_groups=mesh['grp'=2,'aux'=32,'tr'=2] {'aux','tr'}, dimensions={0} | all-to-all | bytes 786432 | tf_op jit(solution)/shard_map/all_to_all | solution.py:267
  61.5 0.0 copy-done.3
  61.5 1.7 %shard_map.88 = (bf16[32,8,384]{2,1,0:T(8,128)(2,1)S(1)}, f32[8,256]{1,0:T(8,128)S(1)}, f32[8,128]{1,0:T(8,128)S(1)}) custom-call(s32[3]{0:T(128)S(1)} %pad_add_fusion.refs_0_.where_ref, bf16[64,8,384]{2,1,0:T(8,128)(2,1)S(1)} %all_to_all.20.arrived_ref, bf16[512,2048]{1,0:T(8,128)(2,1)S(1)} %bitcast.14, f32[2,8,256]{2,1,0:T(8,128)S(1)} %copy-done.8, ...), custom_call_target="tpu_custom_call" | custom-call | tf_op jit(solution)/shard_map/pallas_call | solution.py:279
  63.3 13.1 %all_to_all.21.refs_2_ = bf16[32,8,384]{2,1,0:T(8,128)(2,1)S(1)} all-to-all(bf16[32,8,384]{2,1,0:T(8,128)(2,1)S(1)} %get-tuple-element.5), channel_id=1, replica_groups=mesh['grp'=2,'aux'=32,'tr'=2] {'aux'}, dimensions={0} | all-to-all | bytes 393216 | tf_op jit(solution)/shard_map/all_to_all | solution.py:267
  76.4 0.0 copy-done.5
  76.4 0.0 copy-start.1
  76.4 5.8 %copy-done.1 = bf16[64,256,512]{2,1,0:T(8,128)(2,1)S(1)} copy-done((bf16[64,256,512]{2,1,0:T(8,128)(2,1)S(1)}, bf16[64,256,512]{2,1,0:T(8,128)(2,1)}, u32[]{:S(2)}) %copy-start.1) | copy-done | bytes 16777240
  82.1 8.7 %shard_map.89 = bf16[64,8,384]{2,1,0:T(8,128)(2,1)S(1)} custom-call(s32[3]{0:T(128)S(1)} %pad_add_fusion.refs_0_.where_ref, s32[1]{0:T(128)S(6)} %copy.17.refs_1_, bf16[32,8,384]{2,1,0:T(8,128)(2,1)S(1)} %all_to_all.21.refs_2_, bf16[64,64,64]{2,1,0:T(8,128)(2,1)S(1)} %copy-done.5, bf16[16384,512]{1,0:T(8,128)(2,1)S(1)} %bitcast.12), custom_call_target="tpu_custom_call" | custom-call | tf_op jit(solution)/shard_map/pallas_call | solution.py:236
  90.8 14.1 %all_to_all.22.arrived_ref = bf16[64,8,384]{2,1,0:T(8,128)(2,1)S(1)} all-to-all(bf16[64,8,384]{2,1,0:T(8,128)(2,1)S(1)} %shard_map.89), channel_id=1, replica_groups=mesh['grp'=2,'aux'=32,'tr'=2] {'aux','tr'}, dimensions={0} | all-to-all | bytes 786432 | tf_op jit(solution)/shard_map/all_to_all | solution.py:267
  104.9 0.7 shard_map.90
  105.6 7.7 %all-gather = f32[16,384]{1,0:T(8,128)S(1)} all-gather(f32[8,384]{1,0:T(8,128)S(1)} %pad_maximum_fusion), channel_id=2, replica_groups=mesh['grp'=2,'aux'=32,'tr'=2] {'grp'}, dimensions={0}, use_global_device_ids=true | all-gather | bytes 36864 | tf_op jit(solution)/shard_map/all_gather | solution.py:300
  113.2 0.1 copy.13
  113.3 0.1 copy.14
  113.4 0.7 copy.12
  114.1 0.6 reshape.21
  (6 shorter events, 0.0 us)
Async XLA Ops:
  0.6 1.6 %copy-start.2 = (bf16[2,256,2048]{2,1,0:T(8,128)(2,1)S(1)}, bf16[2,256,2048]{2,1,0:T(8,128)(2,1)}, u32[]{:S(2)}) copy-start(bf16[2,256,2048]{2,1,0:T(8,128)(2,1)} %param.12) | copy-start | bytes 6291460
  2.2 0.7 copy-start.7
  2.9 58.6 %copy-start.3 = (bf16[2,256,2048]{2,1,0:T(8,128)(2,1)S(1)}, bf16[2,256,2048]{2,1,0:T(8,128)(2,1)}, u32[]{:S(2)}) copy-start(bf16[2,256,2048]{2,1,0:T(8,128)(2,1)} %param.12) | copy-start | bytes 6291460
  2.9 73.4 %copy-start.5 = (bf16[64,64,64]{2,1,0:T(8,128)(2,1)S(1)}, bf16[64,64,64]{2,1,0:T(8,128)(2,1)}, u32[]{:S(2)}) copy-start(bf16[64,64,64]{2,1,0:T(8,128)(2,1)} %refs_3_.3) | copy-start | bytes 1572868
  3.3 0.9 copy-start.6
  4.2 25.6 %all-to-all-start = ((bf16[64,8,640]{2,1,0:T(8,128)(2,1)}), bf16[64,8,640]{2,1,0:T(8,128)(2,1)}, u32[]{:S(2)}, u32[]{:S(2)}) async-start(bf16[64,8,640]{2,1,0:T(8,128)(2,1)} %copy-done.6), calls=%async_computation | async-start | bytes 1310720 | tf_op jit(solution)/shard_map/all_to_all | solution.py:267
  29.8 5.8 %copy-start = (bf16[64,256,512]{2,1,0:T(8,128)(2,1)S(1)}, bf16[64,256,512]{2,1,0:T(8,128)(2,1)}, u32[]{:S(2)}) copy-start(bf16[64,256,512]{2,1,0:T(8,128)(2,1)} %param.11) | copy-start | bytes 50331652
  35.6 1.2 %copy-start.4 = (bf16[64,64,64]{2,1,0:T(8,128)(2,1)S(1)}, bf16[64,64,64]{2,1,0:T(8,128)(2,1)}, u32[]{:S(2)}) copy-start(bf16[64,64,64]{2,1,0:T(8,128)(2,1)} %refs_3_.3) | copy-start | bytes 1572868
  36.8 0.7 copy-start.8
  76.4 5.8 %copy-start.1 = (bf16[64,256,512]{2,1,0:T(8,128)(2,1)S(1)}, bf16[64,256,512]{2,1,0:T(8,128)(2,1)}, u32[]{:S(2)}) copy-start(bf16[64,256,512]{2,1,0:T(8,128)(2,1)} %param.11) | copy-start | bytes 50331652

commit v2 on v1

v2 whole, which is shorter than its diff:
```python
import functools

import jax
import jax.numpy as jnp
from jax import lax
from jax.experimental import pallas as pl
from jax.experimental.pallas import tpu as pltpu
from jax.sharding import PartitionSpec as P

V = 64
C = 512
K = 8
HALF = 4
AUX = 32
TR = 2
CB = C // TR
PAIRS = AUX * TR
SLOTS = 64
NAUX = 2048
BLOCK = 8
STEPS = SLOTS // BLOCK
AHEAD = 2
PARTS = 4
TILES = NAUX // 128
F32 = jnp.float32
BF16 = jnp.bfloat16
VMEM = pl.BlockSpec(memory_space=pltpu.VMEM)
SMEM = pl.BlockSpec(memory_space=pltpu.SMEM)
HBM = pl.BlockSpec(memory_space=pltpu.HBM)
NT = (((1,), (1,)), ((), ()))


def stays(x):
    return pltpu.with_memory_space_constraint(x, pltpu.HBM)


def params(mib):
    return pltpu.CompilerParams(vmem_limit_bytes=mib * 2**20)


def dot(a, b):
    return jnp.dot(a, b, preferred_element_type=F32)


def lane_ids(shape):
    return lax.broadcasted_iota(jnp.int32, shape, len(shape) - 1)


def own_rows(core, rows):
    return jnp.where(core == 0, rows[:HALF], rows[HALF:])


def both_halves(rows):
    return jnp.concatenate([rows[:, :CB], rows[:, CB:]], axis=0)


def first_kernel(
    trial_hbm, pair_hbm, cond_hbm, val_hbm, out_ref, trial_ref, gap_ref, pair_ref, cond_ref, val_ref, sems
):
    parts = [pl.ds(NAUX // PARTS * i, NAUX // PARTS) for i in range(PARTS)]
    copies = [
        pltpu.make_async_copy(trial_hbm, trial_ref, sems.at[0]),
        pltpu.make_async_copy(cond_hbm, cond_ref, sems.at[1]),
        pltpu.make_async_copy(val_hbm, val_ref, sems.at[2]),
    ]
    for i in range(PARTS):
        copies.append(pltpu.make_async_copy(pair_hbm.at[:, parts[i]], pair_ref.at[:, parts[i]], sems.at[3 + i]))
    for copy in copies:
        copy.start()
    copies[0].wait()
    wide = jnp.concatenate([trial_ref[v].astype(BF16) for v in range(2)], axis=1)
    for device in range(PAIRS):
        out_ref[device, :, : 2 * CB] = wide
    copies[1].wait()
    copies[2].wait()
    for v in range(2):
        gap_ref[HALF * v : HALF * v + HALF] = jnp.broadcast_to(cond_ref[...] - val_ref[v], (HALF, CB))
    for i in range(PARTS):
        copies[3 + i].wait()
        projection = dot(wide, pair_ref[:, parts[i]]).astype(BF16)
        for tile in range(TILES // PARTS):
            for device in range(4):
                at = 4 * (TILES // PARTS * i + tile) + device
                out_ref[at, :, 2 * CB :] = projection[:, 128 * tile : 128 * tile + 128]


def direct_kernel(first, *refs):
    if first:
        live_ref, arrived_ref, occ_hbm, virt_hbm, trial_ref, gap_ref = refs[:6]
        out_ref, occ_ref, virt_ref, rows_ref, vectors_ref, blended_ref, total_ref, sems = refs[6:]
    else:
        live_ref, arrived_ref, occ_ref, virt_ref = refs[:4]
        out_ref, vectors_ref, blended_ref, total_ref = refs[4:]
    core, aux, tr = lax.axis_index("grp"), lax.axis_index("aux"), lax.axis_index("tr")

    def fetch_occ(step):
        slots = pl.ds(step * BLOCK, BLOCK)
        return pltpu.make_async_copy(occ_hbm.at[slots], occ_ref.at[slots], sems.at[0, step])

    def fetch_virt(step):
        rows = pl.ds(step * BLOCK * CB, BLOCK * CB)
        return pltpu.make_async_copy(virt_hbm.at[rows], virt_ref.at[rows], sems.at[1, step])

    if first:
        for step in range(AHEAD):
            fetch_occ(step).start()
            fetch_virt(step).start()

    row = lax.broadcasted_iota(jnp.int32, (HALF * V, 1), 0)
    if first:
        for a in range(AUX):
            for t in range(TR):
                slab = arrived_ref[2 * a + t, :, : 2 * CB].astype(F32)
                rows_ref[t, 16 * a : 16 * a + 16] = both_halves(slab).astype(BF16)
        chosen = lax.broadcasted_iota(jnp.int32, (HALF * V, K * V), 1)
        wanted = K * (row % V) + HALF * core + row // V
        wide = rows_ref[tr]
    else:
        chosen = lax.broadcasted_iota(jnp.int32, (HALF * V, HALF * V), 1)
        wanted = HALF * (row % V) + row // V
        wide = arrived_ref[:, :, :CB].astype(F32).reshape(HALF * V, CB).astype(BF16)
    vectors_ref[...] = dot((chosen == wanted).astype(BF16), wide).astype(BF16)

    live = live_ref[0]
    slot = lax.broadcasted_iota(jnp.int32, (BLOCK * V, V), 0) // V

    def blend(step):
        occ = occ_ref[BLOCK * step : BLOCK * step + BLOCK].reshape(BLOCK * V, V)
        occ = jnp.where(slot < live - step * BLOCK, occ, jnp.zeros_like(occ))
        for k in range(HALF):
            piece = dot(occ, vectors_ref[V * k : V * k + V]).astype(BF16)
            for p in range(BLOCK):
                blended_ref[step % 2, V * k : V * k + V, CB * p : CB * p + CB] = piece[V * p : V * p + V]

    if first:
        fetch_occ(0).wait()
    blend(0)
    for step in range(STEPS):
        if first:
            fetch_virt(step).wait()
            if step + AHEAD < STEPS:
                fetch_occ(step + AHEAD).start()
                fetch_virt(step + AHEAD).start()
        rows = slice(step * BLOCK * CB, (step + 1) * BLOCK * CB)
        product = dot(blended_ref[step % 2], virt_ref[rows])
        if step + 1 < STEPS:
            if first:
                fetch_occ(step + 1).wait()
            blend(step + 1)
        if step == 0:
            total_ref[...] = product
        else:
            total_ref[...] += product

    lanes = lane_ids((K, 128))
    total = total_ref[...].astype(BF16)
    chosen = lax.broadcasted_iota(jnp.int32, (HALF * V, HALF * V), 1)
    owned = dot((chosen == V * (row % HALF) + row // HALF).astype(BF16), total).astype(BF16).astype(F32)
    if first:
        shares = jnp.zeros((K, HALF * V), F32)
        for t in range(TR):
            product = lax.dot_general(
                rows_ref[t], total[:, CB * t : CB * t + CB], NT, preferred_element_type=F32
            ).reshape(V, K, HALF * V)
            mine = lax.broadcasted_iota(jnp.int32, product.shape, 0)
            theirs = lane_ids(product.shape) % V
            shares += jnp.where(mine == theirs, product, 0.0).sum(axis=0)
        group = lane_ids(shares.shape) // V
        kept = jnp.zeros((K, 128), F32)
        for j in range(HALF):
            column = jnp.where(group == j, shares, 0.0).sum(axis=1, keepdims=True)
            for v in range(2):
                vectors = trial_ref[v]
                other = own_rows(core, vectors)[j : j + 1] * gap_ref[HALF * v : HALF * v + 1]
                column += (vectors * other).sum(axis=1, keepdims=True)
            high = column.astype(BF16).astype(F32)
            kept = jnp.where(lanes % 32 == j, high, kept)
            kept = jnp.where(lanes % 32 == HALF + j, column - high, kept)
        projection = jnp.zeros((K, 128), F32)
        for device in range(PAIRS):
            projection += arrived_ref[device, :, 2 * CB :].astype(F32)
        quarter = (TR * aux + tr) % 4
        extra = jnp.where(lanes // 32 == quarter, projection, kept)
    else:
        extra = jnp.zeros((K, 128), F32)
        for a in range(AUX):
            extra += arrived_ref[a, :, CB:].astype(F32)
    extra = extra.astype(BF16)
    for a in range(AUX):
        for t in range(TR):
            out_ref[2 * a + t, :, :CB] = owned[8 * a : 8 * a + 8, CB * t : CB * t + CB].astype(BF16)
            out_ref[2 * a + t, :, CB:] = extra


def direct_sum(arrived_ref):
    total = jnp.zeros((2 * HALF, CB), F32)
    for device in range(PAIRS):
        total += arrived_ref[device, :, :CB].astype(F32)
    return total


def middle_kernel(
    arrived_ref, pair_ref, trial_ref, gap_ref, out_ref, correction_ref, meet_ref
):
    core = lax.axis_index("grp")
    direct = direct_sum(arrived_ref)
    lanes = lane_ids((K, 128))
    tiles = []
    sums = [jnp.zeros((K, 128), F32) for _ in range(4)]
    for tile in range(TILES):
        whole = jnp.zeros((K, 128), F32)
        for quarter in range(4):
            extra = arrived_ref[4 * tile + quarter, :, CB:].astype(F32)
            whole = jnp.where(lanes // 32 == quarter, extra, whole)
            sums[quarter] += extra
        tiles.append(whole.astype(BF16))
    projection = jnp.concatenate(tiles, axis=1)
    exchange_full = lax.dot_general(projection, pair_ref[...], NT, preferred_element_type=F32)
    mine = own_rows(core, exchange_full)
    exchange = jnp.concatenate([mine[:, :CB], mine[:, CB:]], axis=0)
    shares = jnp.zeros((K, 128), F32)
    for quarter in range(4):
        shares += jnp.where(lanes // 32 == (quarter + 1) % 4, sums[quarter], 0.0)
    meet_exchange = lax.dot_general(projection, projection, NT, preferred_element_type=F32)
    meet = []
    for j in range(HALF):
        column = jnp.where(lanes % 32 % HALF == j, jnp.where(lanes % 32 < K, shares, 0.0), 0.0)
        column = column.sum(axis=1, keepdims=True)
        own = jnp.where(core == 0, meet_exchange[:, j : j + 1], meet_exchange[:, HALF + j : HALF + j + 1])
        meet.append((column + own) / (V * C))
    kept = jnp.zeros((K, 128), F32)
    for j in range(HALF):
        kept = jnp.where(lanes == j, meet[j], kept)
    meet_ref[...] = kept
    gap = gap_ref[...]
    vectors = [trial_ref[v] for v in range(2)]
    trial = jnp.concatenate([own_rows(core, vectors[v]) for v in range(2)], axis=0)
    applied = gap * trial + direct + exchange
    overlap = jnp.concatenate(
        [(vectors[v] * meet[j]).sum(axis=0, keepdims=True) for v in range(2) for j in range(HALF)],
        axis=0,
    )
    correction = (applied - overlap) / gap
    correction_ref[...] = correction
    rounded = correction.astype(BF16)
    wide = jnp.concatenate([correction[:HALF], correction[HALF:]], axis=1)
    wide = jnp.concatenate([wide, jnp.zeros_like(wide)], axis=0).astype(BF16)
    projection = dot(wide, pair_ref[...]).astype(BF16)
    for a in range(AUX):
        tile = a // 2
        out_ref[a, :, :CB] = rounded
        out_ref[a, :, CB:] = projection[:, 128 * tile : 128 * tile + 128]


def last_kernel(arrived_ref, pair_ref, correction_ref, gap_ref, out_ref):
    direct = direct_sum(arrived_ref)
    tiles = []
    for tile in range(TILES):
        whole = arrived_ref[4 * tile, :, CB:].astype(F32) + arrived_ref[4 * tile + 1, :, CB:].astype(F32)
        tiles.append(whole.astype(BF16))
    projection = jnp.concatenate(tiles, axis=1)
    exchange = lax.dot_general(projection, pair_ref[...], NT, preferred_element_type=F32)
    exchange = jnp.concatenate([exchange[:HALF, :CB], exchange[:HALF, CB:]], axis=0)
    out_ref[...] = gap_ref[...] * correction_ref[...] + direct + exchange


def direct_call(first, live, arrived, occ, virt, *local):
    out = jax.ShapeDtypeStruct((PAIRS, 2 * HALF, CB + 128), BF16)
    scratch = [
        pltpu.VMEM((HALF * V, CB), BF16),
        pltpu.VMEM((2, HALF * V, BLOCK * CB), BF16),
        pltpu.VMEM((HALF * V, C), F32),
    ]
    if first:
        scratch = [pltpu.VMEM((TR, K * V, CB), BF16), *scratch, pltpu.SemaphoreType.DMA((2, STEPS))]
    return pl.pallas_call(
        functools.partial(direct_kernel, first),
        in_specs=[SMEM, VMEM, HBM, HBM, VMEM, VMEM] if first else [SMEM, VMEM, VMEM, VMEM],
        out_specs=[VMEM] * 3 if first else VMEM,
        out_shape=[out, jax.typeof(occ), jax.typeof(virt)] if first else out,
        scratch_shapes=scratch,
        compiler_params=params(30 if first else 12),
    )(live, arrived, *((stays(occ), stays(virt)) if first else (occ, virt)), *local)


def body(trial_vectors, energy_val, energy_cond, coef_occ, coef_virt, pair_coef, live_aux):
    pair = pair_coef.reshape(2 * CB, NAUX)
    virt = coef_virt.reshape(SLOTS * CB, C)
    cond = energy_cond.reshape(1, CB)

    def exchange(x, axes):
        return lax.all_to_all(x, axes, split_axis=0, concat_axis=0, tiled=True)

    sent, trial, gap, pair = pl.pallas_call(
        first_kernel,
        in_specs=[HBM] * 4,
        out_specs=[VMEM] * 4,
        out_shape=[
            jax.ShapeDtypeStruct((PAIRS, K, 2 * CB + 128), BF16),
            jax.ShapeDtypeStruct((2, K, CB), F32),
            jax.ShapeDtypeStruct((2 * HALF, CB), F32),
            jax.typeof(pair),
        ],
        scratch_shapes=[
            pltpu.VMEM((1, CB), F32),
            pltpu.SMEM((2,), F32),
            pltpu.SemaphoreType.DMA((3 + PARTS,)),
        ],
        compiler_params=params(8),
    )(*(stays(x) for x in (trial_vectors, pair, cond, energy_val)))
    arrived = exchange(sent, ("aux", "tr"))
    sent, occ, virt = direct_call(True, live_aux, arrived, coef_occ, virt, trial, gap)
    arrived = exchange(sent, ("aux", "tr"))
    sent, correction, meet = pl.pallas_call(
        middle_kernel,
        in_specs=[VMEM] * 4,
        out_specs=[VMEM] * 3,
        out_shape=[
            jax.ShapeDtypeStruct((AUX, 2 * HALF, CB + 128), BF16),
            jax.ShapeDtypeStruct((2 * HALF, CB), F32),
            jax.ShapeDtypeStruct((K, 128), F32),
        ],
        compiler_params=params(8),
    )(arrived, pair, trial, gap)
    arrived = exchange(sent, ("aux",))
    sent = direct_call(False, live_aux, arrived, occ, virt)
    arrived = exchange(sent, ("aux", "tr"))
    applied = pl.pallas_call(
        last_kernel,
        in_specs=[VMEM] * 4,
        out_specs=VMEM,
        out_shape=jax.ShapeDtypeStruct((2 * HALF, CB), F32),
        compiler_params=params(8),
    )(arrived, pair, correction, gap)
    both = lax.all_gather(jnp.concatenate([applied, meet], axis=1), "grp")
    applied = both[:, :, :CB].reshape(2, 2, HALF, CB).transpose(1, 0, 2, 3).reshape(2, K, CB)
    intersection = jnp.concatenate([both[0, :, CB : CB + HALF], both[1, :, CB : CB + HALF]], axis=1)
    return (applied, intersection)


def solution(mesh):
    in_specs = (
        P("aux", None, "tr"),
        P("aux"),
        P("tr"),
        P("aux", None, None),
        P("aux", "tr", None),
        P("aux", "tr", None),
        P("aux"),
    )
    out_specs = (P("aux", None, "tr"), P())
    return jax.shard_map(body, mesh=mesh, in_specs=in_specs, out_specs=out_specs, check_vma=False)
```

time: 115 us -> 98.9 us (0.86)
  local copies, waits for them, and re-layouts: 18.1 us -> 1.46 us
    unnamed x21 -> x3, local copies, waits for them, and re-layouts: 17.5 us -> 0.82 us
  transfers between devices with their start and end apart: 1 -> 1, of which waited for: 1 -> 1; matrix products, arithmetic and copies ran while one was open for 1% -> 0% of each run, Pallas kernels for 0% -> 0%
where the time goes in v2:
time: 98.9 us; the launch traced here: 98.5 us
  blocking collectives  49.2 us (50%)
  Pallas kernels  21.6 us (22%)
  waiting for transfers between devices  12.9 us (13%)
  starting transfers between devices  12 us (12%)
  local copies, waits for them, and re-layouts  1.46 us (1%)
  between operations  1.32 us (1%)
    all_to_all x3, blocking collectives, exchange(): return lax.all_to_all(x, axes, split_axis=0, concat_axis=0, tiled=True)  41.5 us
    pallas_call x2, Pallas kernels, direct_call(): pl.pallas_call(functools.partial(direct_kernel, first), in_specs=[SMEM, V...  17.1 us
    all_to_all x1, waiting for transfers between devices, exchange(): return lax.all_to_all(x, axes, split_axis=0, concat_axis=0, tiled=True)  12.9 us
    all_to_all x1, starting transfers between devices, exchange(): return lax.all_to_all(x, axes, split_axis=0, concat_axis=0, tiled=True)  12 us
    all_gather x1, blocking collectives, body(): both = lax.all_gather(jnp.concatenate([applied, meet], axis=1), 'grp')  7.71 us
    pallas_call x1, Pallas kernels, body(): pl.pallas_call(first_kernel, in_specs=[HBM] * 4, out_specs=[VMEM] * 4, ou...  2.73 us
  transfers between devices with their start and end apart: 1, of which 1 were waited for; matrix products, arithmetic and copies ran while one was open for 0% of the time, Pallas kernels for 0%

profile of v2, /device:TPU:1, one launch (start us, length us, event | category | flops | bytes accessed | tf_op | source)
XLA Modules:
  0.0 98.5 jit_solution(10899038047066010105)
XLA Ops:
  0.6 2.7 %shard_map.86 = (bf16[64,8,640]{2,1,0:T(8,128)(2,1)}, f32[2,8,256]{2,1,0:T(8,128)S(1)}, f32[8,256]{1,0:T(8,128)S(1)}, bf16[512,2048]{1,0:T(8,128)(2,1)S(1)}) custom-call(f32[2,8,256]{2,1,0:T(8,128)} %trial_hbm.1, bf16[512,2048]{1,0:T(8,128)(2,1)} %bitcast.10, f32[1,256]{1,0:T(1,128)} %bitcast.16, f32[2]{0:T(128)} %val_hbm.1), custom_call_target="tpu_custom_call" | custom-call | tf_op jit(solution)/shard_map/pallas_call | solution.py:294
  3.4 12.0 %all-to-all-start = ((bf16[64,8,640]{2,1,0:T(8,128)(2,1)}), bf16[64,8,640]{2,1,0:T(8,128)(2,1)S(1)}, u32[]{:S(2)}, u32[]{:S(2)}) async-start(bf16[64,8,640]{2,1,0:T(8,128)(2,1)} %get-tuple-element.12), calls=%async_computation | async-start | bytes 1310720 | tf_op jit(solution)/shard_map/all_to_all | solution.py:292
  16.0 12.9 %all-to-all-done.refs_1_ = bf16[64,8,640]{2,1,0:T(8,128)(2,1)S(1)} async-done(((bf16[64,8,640]{2,1,0:T(8,128)(2,1)}), bf16[64,8,640]{2,1,0:T(8,128)(2,1)S(1)}, u32[]{:S(2)}, u32[]{:S(2)}) %all-to-all-start) | async-done | bytes 655392 | tf_op jit(solution)/shard_map/all_to_all | solution.py:292
  28.9 10.0 %shard_map.87 = (bf16[64,8,384]{2,1,0:T(8,128)(2,1)S(1)}, bf16[64,64,64]{2,1,0:T(8,128)(2,1)S(1)}, bf16[16384,512]{1,0:T(8,128)(2,1)S(1)}) custom-call(s32[1]{0:T(128)S(6)} %copy.17.refs_0_, bf16[64,8,640]{2,1,0:T(8,128)(2,1)S(1)} %all-to-all-done.refs_1_, bf16[64,64,64]{2,1,0:T(8,128)(2,1)} %refs_2_.1, bf16[16384,512]{1,0:T(8,128)(2,1)} %bitcast.9, ...), custom_call_target="tpu_custom_call" | custom-call | tf_op jit(solution)/shard_map/pallas_call | solution.py:276
  38.9 14.3 %all_to_all.20.arrived_ref = bf16[64,8,384]{2,1,0:T(8,128)(2,1)S(1)} all-to-all(bf16[64,8,384]{2,1,0:T(8,128)(2,1)S(1)} %get-tuple-element.15), channel_id=1, replica_groups=mesh['grp'=2,'aux'=32,'tr'=2] {'aux','tr'}, dimensions={0} | all-to-all | bytes 786432 | tf_op jit(solution)/shard_map/all_to_all | solution.py:292
  53.2 1.2 %shard_map.88 = (bf16[32,8,384]{2,1,0:T(8,128)(2,1)S(1)}, f32[8,256]{1,0:T(8,128)S(1)}, f32[8,128]{1,0:T(8,128)S(1)}) custom-call(bf16[64,8,384]{2,1,0:T(8,128)(2,1)S(1)} %all_to_all.20.arrived_ref, bf16[512,2048]{1,0:T(8,128)(2,1)S(1)} %get-tuple-element.16.pair_ref, f32[2,8,256]{2,1,0:T(8,128)S(1)} %get-tuple-element.13.refs_4_.trial_ref, ...), custom_call_target="tpu_custom_call" | custom-call | tf_op jit(solution)/shard_map/pallas_call | solution.py:314
  54.4 13.0 %all_to_all.21.refs_1_ = bf16[32,8,384]{2,1,0:T(8,128)(2,1)S(1)} all-to-all(bf16[32,8,384]{2,1,0:T(8,128)(2,1)S(1)} %get-tuple-element.17), channel_id=1, replica_groups=mesh['grp'=2,'aux'=32,'tr'=2] {'aux'}, dimensions={0} | all-to-all | bytes 393216 | tf_op jit(solution)/shard_map/all_to_all | solution.py:292
  67.4 7.0 %shard_map.89 = bf16[64,8,384]{2,1,0:T(8,128)(2,1)S(1)} custom-call(s32[1]{0:T(128)S(6)} %copy.17.refs_0_, bf16[32,8,384]{2,1,0:T(8,128)(2,1)S(1)} %all_to_all.21.refs_1_, bf16[64,64,64]{2,1,0:T(8,128)(2,1)S(1)} %get-tuple-element.18.refs_2_, bf16[16384,512]{1,0:T(8,128)(2,1)S(1)} %get-tuple-element.19.refs_3_), custom_call_target="tpu_custom_call" | custom-call | tf_op jit(solution)/shard_map/pallas_call | solution.py:276
  74.5 14.1 %all_to_all.22.arrived_ref = bf16[64,8,384]{2,1,0:T(8,128)(2,1)S(1)} all-to-all(bf16[64,8,384]{2,1,0:T(8,128)(2,1)S(1)} %shard_map.89), channel_id=1, replica_groups=mesh['grp'=2,'aux'=32,'tr'=2] {'aux','tr'}, dimensions={0} | all-to-all | bytes 786432 | tf_op jit(solution)/shard_map/all_to_all | solution.py:292
  88.6 0.7 shard_map.90
  89.3 7.7 %all-gather = f32[16,384]{1,0:T(8,128)S(1)} all-gather(f32[8,384]{1,0:T(8,128)S(1)} %pad_maximum_fusion), channel_id=2, replica_groups=mesh['grp'=2,'aux'=32,'tr'=2] {'grp'}, dimensions={0}, use_global_device_ids=true | all-gather | bytes 36864 | tf_op jit(solution)/shard_map/all_gather | solution.py:335
  97.0 0.6 reshape.23
  97.6 0.1 copy.13
  97.7 0.1 copy.14
  97.8 0.7 copy.12
  (6 shorter events, 0.0 us)
Async XLA Ops:
  3.4 25.5 %all-to-all-start = ((bf16[64,8,640]{2,1,0:T(8,128)(2,1)}), bf16[64,8,640]{2,1,0:T(8,128)(2,1)S(1)}, u32[]{:S(2)}, u32[]{:S(2)}) async-start(bf16[64,8,640]{2,1,0:T(8,128)(2,1)} %get-tuple-element.12), calls=%async_computation | async-start | bytes 1310720 | tf_op jit(solution)/shard_map/all_to_all | solution.py:292

commit v3 on v2

--- a/solution.py
+++ b/solution.py
@@ -19,8 +19,8 @@
 NAUX = 2048
 BLOCK = 8
 STEPS = SLOTS // BLOCK
-AHEAD = 2
 PARTS = 4
+UNTIL_DIRECT = 2 * 10**10
 TILES = NAUX // 128
 F32 = jnp.float32
 BF16 = jnp.bfloat16
@@ -55,7 +55,7 @@
 
 
 def first_kernel(
-    trial_hbm, pair_hbm, cond_hbm, val_hbm, out_ref, trial_ref, gap_ref, pair_ref, cond_ref, val_ref, sems
+    live_ref, trial_hbm, pair_hbm, cond_hbm, val_hbm, out_ref, trial_ref, gap_ref, pair_ref, cond_ref, val_ref, sems
 ):
     parts = [pl.ds(NAUX // PARTS * i, NAUX // PARTS) for i in range(PARTS)]
     copies = [
@@ -86,25 +86,12 @@
 
 def direct_kernel(first, *refs):
     if first:
-        live_ref, arrived_ref, occ_hbm, virt_hbm, trial_ref, gap_ref = refs[:6]
-        out_ref, occ_ref, virt_ref, rows_ref, vectors_ref, blended_ref, total_ref, sems = refs[6:]
+        live_ref, arrived_ref, occ_ref, virt_ref, trial_ref, gap_ref = refs[:6]
+        out_ref, rows_ref, vectors_ref, blended_ref, total_ref = refs[6:]
     else:
         live_ref, arrived_ref, occ_ref, virt_ref = refs[:4]
         out_ref, vectors_ref, blended_ref, total_ref = refs[4:]
     core, aux, tr = lax.axis_index("grp"), lax.axis_index("aux"), lax.axis_index("tr")
-
-    def fetch_occ(step):
-        slots = pl.ds(step * BLOCK, BLOCK)
-        return pltpu.make_async_copy(occ_hbm.at[slots], occ_ref.at[slots], sems.at[0, step])
-
-    def fetch_virt(step):
-        rows = pl.ds(step * BLOCK * CB, BLOCK * CB)
-        return pltpu.make_async_copy(virt_hbm.at[rows], virt_ref.at[rows], sems.at[1, step])
-
-    if first:
-        for step in range(AHEAD):
-            fetch_occ(step).start()
-            fetch_virt(step).start()
 
     row = lax.broadcasted_iota(jnp.int32, (HALF * V, 1), 0)
     if first:
@@ -132,20 +119,11 @@
             for p in range(BLOCK):
                 blended_ref[step % 2, V * k : V * k + V, CB * p : CB * p + CB] = piece[V * p : V * p + V]
 
-    if first:
-        fetch_occ(0).wait()
     blend(0)
     for step in range(STEPS):
-        if first:
-            fetch_virt(step).wait()
-            if step + AHEAD < STEPS:
-                fetch_occ(step + AHEAD).start()
-                fetch_virt(step + AHEAD).start()
         rows = slice(step * BLOCK * CB, (step + 1) * BLOCK * CB)
         product = dot(blended_ref[step % 2], virt_ref[rows])
         if step + 1 < STEPS:
-            if first:
-                fetch_occ(step + 1).wait()
             blend(step + 1)
         if step == 0:
             total_ref[...] = product
@@ -272,15 +250,15 @@
         pltpu.VMEM((HALF * V, C), F32),
     ]
     if first:
-        scratch = [pltpu.VMEM((TR, K * V, CB), BF16), *scratch, pltpu.SemaphoreType.DMA((2, STEPS))]
+        scratch = [pltpu.VMEM((TR, K * V, CB), BF16), *scratch]
     return pl.pallas_call(
         functools.partial(direct_kernel, first),
-        in_specs=[SMEM, VMEM, HBM, HBM, VMEM, VMEM] if first else [SMEM, VMEM, VMEM, VMEM],
-        out_specs=[VMEM] * 3 if first else VMEM,
-        out_shape=[out, jax.typeof(occ), jax.typeof(virt)] if first else out,
+        in_specs=[SMEM] + [VMEM] * (5 if first else 3),
+        out_specs=VMEM,
+        out_shape=out,
         scratch_shapes=scratch,
-        compiler_params=params(30 if first else 12),
-    )(live, arrived, *((stays(occ), stays(virt)) if first else (occ, virt)), *local)
+        compiler_params=params(12),
+    )(live, arrived, occ, virt, *local)
 
 
 def body(trial_vectors, energy_val, energy_cond, coef_occ, coef_virt, pair_coef, live_aux):
@@ -293,7 +271,7 @@
 
     sent, trial, gap, pair = pl.pallas_call(
         first_kernel,
-        in_specs=[HBM] * 4,
+        in_specs=[SMEM] + [HBM] * 4,
         out_specs=[VMEM] * 4,
         out_shape=[
             jax.ShapeDtypeStruct((PAIRS, K, 2 * CB + 128), BF16),
@@ -306,10 +284,11 @@
             pltpu.SMEM((2,), F32),
             pltpu.SemaphoreType.DMA((3 + PARTS,)),
         ],
+        cost_estimate=pl.CostEstimate(flops=UNTIL_DIRECT, bytes_accessed=2 * pair.size, transcendentals=0),
         compiler_params=params(8),
-    )(*(stays(x) for x in (trial_vectors, pair, cond, energy_val)))
+    )(live_aux, *(stays(x) for x in (trial_vectors, pair, cond, energy_val)))
     arrived = exchange(sent, ("aux", "tr"))
-    sent, occ, virt = direct_call(True, live_aux, arrived, coef_occ, virt, trial, gap)
+    sent = direct_call(True, live_aux, arrived, coef_occ, virt, trial, gap)
     arrived = exchange(sent, ("aux", "tr"))
     sent, correction, meet = pl.pallas_call(
         middle_kernel,
@@ -323,7 +302,7 @@
         compiler_params=params(8),
     )(arrived, pair, trial, gap)
     arrived = exchange(sent, ("aux",))
-    sent = direct_call(False, live_aux, arrived, occ, virt)
+    sent = direct_call(False, live_aux, arrived, coef_occ, virt)
     arrived = exchange(sent, ("aux", "tr"))
     applied = pl.pallas_call(
         last_kernel,

time: 98.9 us -> 96.4 us (0.975)
  blocking collectives: 49.2 us -> 74.7 us
  waiting for transfers between devices: 12.9 us -> 0 us
  starting transfers between devices: 12 us -> 0 us
  Pallas kernels: 21.6 us -> 18.5 us
    all_to_all x3 -> x4, blocking collectives: 41.5 us -> 67 us  [exchange(): return lax.all_to_all(x, axes, split_axis=0, concat_axis=0, tiled=True)]
    all_to_all x1 -> x0, waiting for transfers between devices: 12.9 us -> none  [exchange(): return lax.all_to_all(x, axes, split_axis=0, concat_axis=0, tiled=True)]
    all_to_all x1 -> x0, starting transfers between devices: 12 us -> none  [exchange(): return lax.all_to_all(x, axes, split_axis=0, concat_axis=0, tiled=True)]
    pallas_call x3, Pallas kernels: 19.8 us -> 16.6 us  [the longest x2 14.6 us: direct_call(): pl.pallas_call(functools.partial(direct_kernel, first), in_specs=[SMEM] +...]
  transfers between devices with their start and end apart: 1 -> 0, of which waited for: 1 -> 0; matrix products, arithmetic and copies ran while one was open for 0% -> 0% of each run, Pallas kernels for 0% -> 0%
where the time goes in v3:
time: 96.4 us; the launch traced here: 96.1 us
  blocking collectives  74.7 us (77%)
  Pallas kernels  18.5 us (19%)
  local copies, waits for them, and re-layouts  1.49 us (2%)
  between operations  1.38 us (1%)
    all_to_all x4, blocking collectives, exchange(): return lax.all_to_all(x, axes, split_axis=0, concat_axis=0, tiled=True)  67 us
    pallas_call x2, Pallas kernels, direct_call(): pl.pallas_call(functools.partial(direct_kernel, first), in_specs=[SMEM] +...  14.6 us
    all_gather x1, blocking collectives, body(): both = lax.all_gather(jnp.concatenate([applied, meet], axis=1), 'grp')  7.72 us
    pallas_call x1, Pallas kernels, body(): pl.pallas_call(first_kernel, in_specs=[SMEM] + [HBM] * 4, out_specs=[VMEM...  2.05 us

profile of v3, /device:TPU:1, one launch (start us, length us, event | category | flops | bytes accessed | tf_op | source)
XLA Modules:
  0.0 96.1 jit_solution(7179288384450014433)
XLA Ops:
  1.3 0.0 slice-start
  1.3 0.0 slice-start.1
  1.3 0.0 slice-start.2
  1.3 0.0 slice-start.3
  1.3 0.0 copy-start
  1.3 2.0 %shard_map.86 = (bf16[64,8,640]{2,1,0:T(8,128)(2,1)S(1)}, f32[2,8,256]{2,1,0:T(8,128)S(1)}, f32[8,256]{1,0:T(8,128)S(1)}, bf16[512,2048]{1,0:T(8,128)(2,1)S(1)}) custom-call(s32[1]{0:T(128)S(6)} %copy.17.live_ref.refs_0_, f32[2,8,256]{2,1,0:T(8,128)} %trial_hbm.1, bf16[512,2048]{1,0:T(8,128)(2,1)} %bitcast.18, f32[1,256]{1,0:T(1,128)} %bitcast.19, f32[2]{0:T(128)} %val_hbm.1), custom_call_target="tpu_custom_call" | custom-call | flops 20000000000 | bytes 2097152 | tf_op jit(solution)/shard_map/pallas_call | solution.py:272
  3.4 25.5 %all_to_all.20.refs_1_ = bf16[64,8,640]{2,1,0:T(8,128)(2,1)S(1)} all-to-all(bf16[64,8,640]{2,1,0:T(8,128)(2,1)S(1)} %get-tuple-element.9), channel_id=1, replica_groups=mesh['grp'=2,'aux'=32,'tr'=2] {'aux','tr'}, dimensions={0} | all-to-all | bytes 1310720 | tf_op jit(solution)/shard_map/all_to_all | solution.py:270
  28.9 0.0 slice-done
  28.9 0.0 slice-done.1
  28.9 0.0 slice-done.2
  28.9 0.0 slice-done.3
  29.0 0.0 copy-done
  29.0 7.5 %shard_map.87 = bf16[64,8,384]{2,1,0:T(8,128)(2,1)S(1)} custom-call(s32[1]{0:T(128)S(6)} %copy.17.live_ref.refs_0_, bf16[64,8,640]{2,1,0:T(8,128)(2,1)S(1)} %all_to_all.20.refs_1_, bf16[64,64,64]{2,1,0:T(8,128)(2,1)S(1)} %copy-done, bf16[16384,512]{1,0:T(8,128)(2,1)S(1)} %bitcast.11, f32[2,8,256]{2,1,0:T(8,128)S(1)} %get-tuple-element.10.refs_4_.trial_ref, ...), custom_call_target="tpu_custom_call" | custom-call | tf_op jit(solution)/shard_map/pallas_call | solution.py:254
  36.5 14.3 %all_to_all.21.arrived_ref = bf16[64,8,384]{2,1,0:T(8,128)(2,1)S(1)} all-to-all(bf16[64,8,384]{2,1,0:T(8,128)(2,1)S(1)} %shard_map.87), channel_id=1, replica_groups=mesh['grp'=2,'aux'=32,'tr'=2] {'aux','tr'}, dimensions={0} | all-to-all | bytes 786432 | tf_op jit(solution)/shard_map/all_to_all | solution.py:270
  50.8 1.2 %shard_map.88 = (bf16[32,8,384]{2,1,0:T(8,128)(2,1)S(1)}, f32[8,256]{1,0:T(8,128)S(1)}, f32[8,128]{1,0:T(8,128)S(1)}) custom-call(bf16[64,8,384]{2,1,0:T(8,128)(2,1)S(1)} %all_to_all.21.arrived_ref, bf16[512,2048]{1,0:T(8,128)(2,1)S(1)} %get-tuple-element.12.pair_ref, f32[2,8,256]{2,1,0:T(8,128)S(1)} %get-tuple-element.10.refs_4_.trial_ref, ...), custom_call_target="tpu_custom_call" | custom-call | tf_op jit(solution)/shard_map/pallas_call | solution.py:293
  52.0 13.0 %all_to_all.22.refs_1_ = bf16[32,8,384]{2,1,0:T(8,128)(2,1)S(1)} all-to-all(bf16[32,8,384]{2,1,0:T(8,128)(2,1)S(1)} %get-tuple-element.13), channel_id=1, replica_groups=mesh['grp'=2,'aux'=32,'tr'=2] {'aux'}, dimensions={0} | all-to-all | bytes 393216 | tf_op jit(solution)/shard_map/all_to_all | solution.py:270
  65.1 7.0 %shard_map.89 = bf16[64,8,384]{2,1,0:T(8,128)(2,1)S(1)} custom-call(s32[1]{0:T(128)S(6)} %copy.17.live_ref.refs_0_, bf16[32,8,384]{2,1,0:T(8,128)(2,1)S(1)} %all_to_all.22.refs_1_, bf16[64,64,64]{2,1,0:T(8,128)(2,1)S(1)} %copy-done, bf16[16384,512]{1,0:T(8,128)(2,1)S(1)} %bitcast.12), custom_call_target="tpu_custom_call" | custom-call | tf_op jit(solution)/shard_map/pallas_call | solution.py:254
  72.1 14.1 %all_to_all.23.arrived_ref = bf16[64,8,384]{2,1,0:T(8,128)(2,1)S(1)} all-to-all(bf16[64,8,384]{2,1,0:T(8,128)(2,1)S(1)} %shard_map.89), channel_id=1, replica_groups=mesh['grp'=2,'aux'=32,'tr'=2] {'aux','tr'}, dimensions={0} | all-to-all | bytes 786432 | tf_op jit(solution)/shard_map/all_to_all | solution.py:270
  86.2 0.7 shard_map.90
  86.9 7.7 %all-gather = f32[16,384]{1,0:T(8,128)S(1)} all-gather(f32[8,384]{1,0:T(8,128)S(1)} %pad_maximum_fusion), channel_id=2, replica_groups=mesh['grp'=2,'aux'=32,'tr'=2] {'grp'}, dimensions={0}, use_global_device_ids=true | all-gather | bytes 36864 | tf_op jit(solution)/shard_map/all_gather | solution.py:314
  94.6 0.6 reshape.23
  95.2 0.1 copy.13
  95.3 0.1 copy.14
  95.4 0.7 copy.12
  (7 shorter events, 0.0 us)
Async XLA Ops:
  1.3 27.7 %slice-start = ((s8[16777216]{0:T(1024)(128)(4,1)}), s8[4194304]{0:T(1024)(128)(4,1)S(1)}, s32[]{:S(2)}) async-start(s8[16777216]{0:T(1024)(128)(4,1)} %bitcast.9), calls=%async_computation.4 | async-start | bytes 8388608
  1.3 27.6 %slice-start.1 = ((s8[16777216]{0:T(1024)(128)(4,1)}), s8[4194304]{0:T(1024)(128)(4,1)S(1)}, s32[]{:S(2)}) async-start(s8[16777216]{0:T(1024)(128)(4,1)} %bitcast.9), calls=%async_computation.5 | async-start | bytes 8388608
  1.3 27.6 %slice-start.2 = ((s8[16777216]{0:T(1024)(128)(4,1)}), s8[4194304]{0:T(1024)(128)(4,1)S(1)}, s32[]{:S(2)}) async-start(s8[16777216]{0:T(1024)(128)(4,1)} %bitcast.9), calls=%async_computation.6 | async-start | bytes 8388608
  1.3 27.6 %slice-start.3 = ((s8[16777216]{0:T(1024)(128)(4,1)}), s8[4194304]{0:T(1024)(128)(4,1)S(1)}, s32[]{:S(2)}) async-start(s8[16777216]{0:T(1024)(128)(4,1)} %bitcast.9), calls=%async_computation.7 | async-start | bytes 8388608
  1.3 27.6 %copy-start = (bf16[64,64,64]{2,1,0:T(8,128)(2,1)S(1)}, bf16[64,64,64]{2,1,0:T(8,128)(2,1)}, u32[]{:S(2)}) copy-start(bf16[64,64,64]{2,1,0:T(8,128)(2,1)} %refs_2_.3) | copy-start | bytes 1572868

commit v4 on v3

v4 whole, which is shorter than its diff:
```python
import functools

import jax
import jax.numpy as jnp
from jax import lax
from jax.experimental import pallas as pl
from jax.experimental.pallas import tpu as pltpu
from jax.sharding import Mesh
from jax.sharding import PartitionSpec as P

V = 64
C = 512
K = 8
SPLIT = 3
SEATS = 5
HALF = 4
AUX = 32
TR = 2
CB = C // TR
PAIRS = AUX * TR
ALL = ("zh", "tr", "y", "x")
SAME_TR = ("zh", "y", "x")
SLOTS = 64
NAUX = 2048
BLOCK = 8
STEPS = SLOTS // BLOCK
PARTS = 4
UNTIL_DIRECT = 2 * 10**10
TILES = NAUX // 128
F32 = jnp.float32
BF16 = jnp.bfloat16
VMEM = pl.BlockSpec(memory_space=pltpu.VMEM)
SMEM = pl.BlockSpec(memory_space=pltpu.SMEM)
HBM = pl.BlockSpec(memory_space=pltpu.HBM)
NT = (((1,), (1,)), ((), ()))


def place(a, t):
    y, zh, x = a // 8, a // 4 % 2, a % 4
    return zh * 32 + t * 16 + y * 4 + x


def place_same_tr(a):
    y, zh, x = a // 8, a // 4 % 2, a % 4
    return zh * 16 + y * 4 + x


def stays(x):
    return pltpu.with_memory_space_constraint(x, pltpu.HBM)


def params(mib):
    return pltpu.CompilerParams(vmem_limit_bytes=mib * 2**20)


def dot(a, b):
    return jnp.dot(a, b, preferred_element_type=F32)


def lane_ids(shape):
    return lax.broadcasted_iota(jnp.int32, shape, len(shape) - 1)


def row_ids(shape):
    return lax.broadcasted_iota(jnp.int32, shape, 0)


def own_seats(core, rows):
    return jnp.where(core == 0, rows[:SEATS], rows[K - SEATS :])


def both_halves(rows):
    return jnp.concatenate([rows[:, :CB], rows[:, CB:]], axis=0)


def first_kernel(
    live_ref, trial_hbm, pair_hbm, cond_hbm, val_hbm, out_ref, trial_ref, gap_ref, pair_ref, cond_ref, val_ref, sems
):
    parts = [pl.ds(NAUX // PARTS * i, NAUX // PARTS) for i in range(PARTS)]
    copies = [
        pltpu.make_async_copy(trial_hbm, trial_ref, sems.at[0]),
        pltpu.make_async_copy(cond_hbm, cond_ref, sems.at[1]),
        pltpu.make_async_copy(val_hbm, val_ref, sems.at[2]),
    ]
    for i in range(PARTS):
        copies.append(pltpu.make_async_copy(pair_hbm.at[:, parts[i]], pair_ref.at[:, parts[i]], sems.at[3 + i]))
    for copy in copies:
        copy.start()
    copies[0].wait()
    wide = jnp.concatenate([trial_ref[v].astype(BF16) for v in range(2)], axis=1)
    for device in range(PAIRS):
        out_ref[device, :, : 2 * CB] = wide
    copies[1].wait()
    copies[2].wait()
    for v in range(2):
        gap_ref[HALF * v : HALF * v + HALF] = jnp.broadcast_to(cond_ref[...] - val_ref[v], (HALF, CB))
    for i in range(PARTS):
        copies[3 + i].wait()
        projection = dot(wide, pair_ref[:, parts[i]]).astype(BF16)
        for tile in range(TILES // PARTS):
            for device in range(4):
                at = 4 * (TILES // PARTS * i + tile) + device
                out_ref[at, :, 2 * CB :] = projection[:, 128 * tile : 128 * tile + 128]


def direct_kernel(first, *refs):
    if first:
        live_ref, arrived_ref, occ_ref, virt_ref, trial_ref, gap_ref, out_ref = refs[:7]
        rows_ref, vectors_ref, blended_ref, total_ref = refs[7:]
    else:
        live_ref, arrived_ref, occ_ref, virt_ref, out_ref = refs[:5]
        vectors_ref, blended_ref, total_ref = refs[5:]
    core, tr, quarter = lax.axis_index("grp"), lax.axis_index("tr"), lax.axis_index("x")

    if first:
        for a in range(AUX):
            for t in range(TR):
                slab = arrived_ref[place(a, t), :, : 2 * CB].astype(F32)
                rows_ref[t, 16 * a : 16 * a + 16] = both_halves(slab).astype(BF16)
        row = row_ids((SEATS * V, 1))
        wanted = K * (row % V) + SPLIT * core + row // V
        chosen = lane_ids((SEATS * V, K * V)) == wanted
        vectors_ref[...] = dot(chosen.astype(BF16), rows_ref[tr]).astype(BF16)
    else:
        tiles = [arrived_ref[place_same_tr(a)].astype(F32) for a in range(AUX)]
        wide = jnp.concatenate(tiles, axis=0).astype(BF16)
        row = row_ids((HALF * V, 1))
        chosen = lane_ids((HALF * V, 8 * AUX)) == HALF * (row % V) + row // V
        vectors_ref[: HALF * V] = dot(chosen.astype(BF16), wide[:, :CB]).astype(BF16)
        row = row_ids((V, 1))
        for h in range(2):
            chosen = lane_ids((V, 8 * AUX)) == 8 * (row // 2) + 2 * h + row % 2
            part = dot(chosen.astype(BF16), wide[:, CB:]).astype(BF16)
            vectors_ref[HALF * V :, 128 * h : 128 * h + 128] = part

    live = live_ref[0]

    def accumulate(seats):
        slot = row_ids((BLOCK * V, V)) // V
        size = seats * V

        def blend(step):
            occ = occ_ref[BLOCK * step : BLOCK * step + BLOCK].reshape(BLOCK * V, V)
            occ = jnp.where(slot < live - step * BLOCK, occ, jnp.zeros_like(occ))
            for k in range(seats):
                piece = dot(occ, vectors_ref[V * k : V * k + V]).astype(BF16)
                for p in range(BLOCK):
                    blended_ref[step % 2, V * k : V * k + V, CB * p : CB * p + CB] = piece[V * p : V * p + V]

        blend(0)
        for step in range(STEPS):
            rows = slice(step * BLOCK * CB, (step + 1) * BLOCK * CB)
            product = dot(blended_ref[step % 2, :size], virt_ref[rows])
            if step + 1 < STEPS:
                blend(step + 1)
            if step == 0:
                total_ref[:size] = product
            else:
                total_ref[:size] += product
        if seats < SEATS:
            total_ref[size:] = jnp.zeros((SEATS * V - size, C), F32)

    @pl.when(core == 0)
    def _():
        accumulate(SPLIT)

    @pl.when(core != 0)
    def _():
        accumulate(SEATS)

    total = total_ref[...].astype(BF16)
    row = row_ids((HALF * V, 1))
    chosen = lane_ids((HALF * V, HALF * V)) == V * (row % HALF) + row // HALF
    owned = dot(chosen.astype(BF16), total[: HALF * V]).astype(BF16).astype(F32)
    late = [
        jnp.concatenate([total[HALF * V :, CB * t + 128 * h : CB * t + 128 * h + 128] for t in range(TR)], axis=1)
        for h in range(2)
    ]
    row = row_ids((8 * AUX, 1))
    chosen = lane_ids((8 * AUX, 2 * V)) == V * (row % 8 // 2) + 2 * (row // 8) + row % 2
    chosen = jnp.where(row % 8 < 4, chosen.astype(F32), 0.0)
    late = dot(chosen.astype(BF16), jnp.concatenate(late, axis=0))

    lanes = lane_ids((K, 128))
    if first:
        shares = jnp.zeros((K, SEATS * V), F32)
        for t in range(TR):
            product = lax.dot_general(
                rows_ref[t], total[:, CB * t : CB * t + CB], NT, preferred_element_type=F32
            ).reshape(V, K, SEATS * V)
            theirs = lane_ids(product.shape) % V
            shares += jnp.where(row_ids(product.shape) == theirs, product, 0.0).sum(axis=0)
        group = lane_ids(shares.shape) // V
        kept = jnp.zeros((K, 128), F32)
        for j in range(SEATS):
            column = jnp.where(group == j, shares, 0.0).sum(axis=1, keepdims=True)
            for v in range(2):
                vectors = trial_ref[v]
                other = own_seats(core, vectors)[j : j + 1] * gap_ref[HALF * v : HALF * v + 1]
                column += (vectors * other).sum(axis=1, keepdims=True)
            high = column.astype(BF16).astype(F32)
            kept = jnp.where(lanes % 32 == j, high, kept)
            kept = jnp.where(lanes % 32 == 8 + j, column - high, kept)
        projection = jnp.zeros((K, 128), F32)
        for device in range(PAIRS):
            projection += arrived_ref[device, :, 2 * CB :].astype(F32)
        extra = jnp.where(lanes // 32 == quarter, projection, kept)
        near = lax.rem(lanes // 32 - quarter + 4, 4) < 2
        extra = jnp.where(near, pltpu.roll(extra, 4, 0), pltpu.roll(extra, 64, 1))
    else:
        extra = jnp.zeros((K, 128), F32)
        for tile in tiles:
            extra += tile[:, CB:]
    extra = jnp.where(row_ids((K, 128)) >= 4, extra, 0.0)
    for a in range(AUX):
        for t in range(TR):
            out_ref[place(a, t), :, :CB] = owned[8 * a : 8 * a + 8, CB * t : CB * t + CB].astype(BF16)
            part = late[8 * a : 8 * a + 8, 128 * t : 128 * t + 128] + extra
            out_ref[place(a, t), :, CB:] = part.astype(BF16)


def direct_sum(arrived_ref):
    total = jnp.zeros((8, CB + 128), F32)
    for device in range(PAIRS):
        total += arrived_ref[device].astype(F32)
    return total[:, :CB], jnp.concatenate([total[:2, CB:], total[2:4, CB:]], axis=1)


def seat_rows(own):
    rows = jnp.concatenate([own[:HALF, :CB], own[:HALF, CB:]], axis=0)
    return rows, jnp.concatenate([own[HALF:SEATS, :CB], own[HALF:SEATS, CB:]], axis=0)


def middle_kernel(
    arrived_ref, pair_ref, trial_ref, gap_ref, out_ref, correction_ref, meet_ref
):
    core = lax.axis_index("grp")
    direct = direct_sum(arrived_ref)
    lanes, rows = lane_ids((K, 128)), row_ids((K, 128))
    tiles = []
    sums = [jnp.zeros((K, 128), F32) for _ in range(4)]
    for tile in range(TILES):
        low = high = jnp.zeros((K, 128), F32)
        for quarter in range(4):
            extra = arrived_ref[4 * tile + quarter, :, CB:].astype(F32)
            low = jnp.where(lanes // 32 == quarter, extra, low)
            high = jnp.where(lanes // 32 == (quarter + 2) % 4, extra, high)
            sums[quarter] += extra
        whole = jnp.where(rows < 4, pltpu.roll(low, 4, 0), pltpu.roll(high, 64, 1))
        tiles.append(whole.astype(BF16))
    projection = jnp.concatenate(tiles, axis=1)
    exchange = lax.dot_general(projection, pair_ref[...], NT, preferred_element_type=F32)
    exchange = seat_rows(own_seats(core, exchange))
    low = high = jnp.zeros((K, 128), F32)
    for quarter in range(4):
        low = jnp.where(lanes // 32 == (quarter + 1) % 4, sums[quarter], low)
        high = jnp.where(lanes // 32 == (quarter + 3) % 4, sums[quarter], high)
    shares = jnp.where(rows < 4, pltpu.roll(low, 4, 0), high)
    meet_exchange = lax.dot_general(projection, projection, NT, preferred_element_type=F32)
    meet = []
    kept = jnp.zeros((K, 128), F32)
    for j in range(SEATS):
        mine = (lanes % 32 == j) | (lanes % 32 == 8 + j)
        column = jnp.where(mine, shares, 0.0).sum(axis=1, keepdims=True)
        other = K - SEATS + j
        column += jnp.where(core == 0, meet_exchange[:, j : j + 1], meet_exchange[:, other : other + 1])
        meet.append(column / (V * C))
        kept = jnp.where(lanes == j, meet[j], kept)
    meet_ref[...] = kept
    vectors = [trial_ref[v] for v in range(2)]
    trial = seat_rows(jnp.concatenate([own_seats(core, vectors[v]) for v in range(2)], axis=1))
    gaps = (gap_ref[...], jnp.concatenate([gap_ref[:1], gap_ref[HALF : HALF + 1]], axis=0))
    seats = (range(HALF), range(HALF, SEATS))
    correction = []
    for i in range(2):
        applied = gaps[i] * trial[i] + direct[i] + exchange[i]
        overlap = [(vectors[v] * meet[j]).sum(axis=0, keepdims=True) for v in range(2) for j in seats[i]]
        correction.append((applied - jnp.concatenate(overlap, axis=0)) / gaps[i])
    rows4, rows1 = correction
    correction_ref[:8] = rows4
    correction_ref[8:] = jnp.concatenate([rows1, jnp.zeros((6, CB), F32)], axis=0)
    wide = jnp.concatenate(
        [
            jnp.concatenate([rows4[:HALF], rows4[HALF:]], axis=1),
            jnp.concatenate([rows1[:1], rows1[1:]], axis=1),
            jnp.zeros((K - SEATS, 2 * CB), F32),
        ],
        axis=0,
    )
    projection = dot(wide.astype(BF16), pair_ref[...]).astype(BF16).astype(F32)
    rounded = rows4.astype(BF16)
    late = jnp.concatenate([rows1[:, :128], rows1[:, 128:]], axis=0)
    for tile in range(TILES):
        part = projection[:, 128 * tile : 128 * tile + 128]
        here = jnp.concatenate([late, part[:HALF]], axis=0)
        away = jnp.broadcast_to(pltpu.roll(part, 64, 1)[HALF:SEATS], (4, 128))
        away = jnp.concatenate([late, away], axis=0)
        for half in range(2):
            out_ref[2 * tile + half, :, :CB] = rounded
            both = jnp.where(lanes // 64 == half, here, away)
            out_ref[2 * tile + half, :, CB:] = both.astype(BF16)


def last_kernel(arrived_ref, pair_ref, correction_ref, gap_ref, meet_ref, out_ref):
    direct = direct_sum(arrived_ref)
    lanes, rows = lane_ids((K, 128)), row_ids((K, 128))
    tiles = []
    for tile in range(TILES):
        at = tile // 8 * 32 + 2 * tile % 16
        parts = [
            arrived_ref[at + half, :, CB:].astype(F32) + arrived_ref[at + 16 + half, :, CB:].astype(F32)
            for half in range(2)
        ]
        here = jnp.where(lanes < 64, parts[0], parts[1])
        away = pltpu.roll(jnp.where(lanes < 64, parts[1], parts[0]), 64, 1)
        tiles.append(jnp.where(rows >= 4, here, pltpu.roll(away, 4, 0)).astype(BF16))
    projection = jnp.concatenate(tiles, axis=1)
    exchange = lax.dot_general(projection, pair_ref[...], NT, preferred_element_type=F32)
    exchange = seat_rows(jnp.concatenate([exchange[HALF:], exchange[:1]], axis=0))
    out_ref[:, :CB] = gap_ref[...] * correction_ref[:8] + direct[0] + exchange[0]
    out_ref[:, CB : CB + 128] = meet_ref[...]
    gap = jnp.concatenate([gap_ref[:1], gap_ref[HALF : HALF + 1]], axis=0)
    late = gap * correction_ref[8:10] + direct[1] + exchange[1]
    out_ref[:, CB + 128 :] = jnp.concatenate([late, jnp.zeros((6, CB), F32)], axis=0)


def join_kernel(both_ref, applied_ref, meet_ref):
    for v in range(2):
        rows = [
            both_ref[0, HALF * v : HALF * v + SPLIT, :CB],
            both_ref[1, HALF * v : HALF * v + HALF, :CB],
            both_ref[1, v : v + 1, CB + 128 :],
        ]
        applied_ref[v] = jnp.concatenate(rows, axis=0)
    columns = [both_ref[0, :, CB : CB + SPLIT], both_ref[1, :, CB : CB + SEATS]]
    meet_ref[...] = jnp.concatenate(columns, axis=1)


def direct_call(first, live, arrived, occ, virt, *local):
    out = jax.ShapeDtypeStruct((PAIRS, 8, CB + 128), BF16)
    scratch = [
        pltpu.VMEM((SEATS * V, CB), BF16),
        pltpu.VMEM((2, SEATS * V, BLOCK * CB), BF16),
        pltpu.VMEM((SEATS * V, C), F32),
    ]
    if first:
        scratch = [pltpu.VMEM((TR, K * V, CB), BF16), *scratch]
    return pl.pallas_call(
        functools.partial(direct_kernel, first),
        in_specs=[SMEM] + [VMEM] * (5 if first else 3),
        out_specs=VMEM,
        out_shape=out,
        scratch_shapes=scratch,
        compiler_params=params(12),
    )(live, arrived, occ, virt, *local)


def body(trial_vectors, energy_val, energy_cond, coef_occ, coef_virt, pair_coef, live_aux):
    pair = pair_coef.reshape(2 * CB, NAUX)
    virt = coef_virt.reshape(SLOTS * CB, C)
    cond = energy_cond.reshape(1, CB)

    def exchange(x, axes):
        return lax.all_to_all(x, axes, split_axis=0, concat_axis=0, tiled=True)

    sent, trial, gap, pair = pl.pallas_call(
        first_kernel,
        in_specs=[SMEM] + [HBM] * 4,
        out_specs=[VMEM] * 4,
        out_shape=[
            jax.ShapeDtypeStruct((PAIRS, K, 2 * CB + 128), BF16),
            jax.ShapeDtypeStruct((2, K, CB), F32),
            jax.ShapeDtypeStruct((2 * HALF, CB), F32),
            jax.typeof(pair),
        ],
        scratch_shapes=[
            pltpu.VMEM((1, CB), F32),
            pltpu.SMEM((2,), F32),
            pltpu.SemaphoreType.DMA((3 + PARTS,)),
        ],
        cost_estimate=pl.CostEstimate(flops=UNTIL_DIRECT, bytes_accessed=2 * pair.size, transcendentals=0),
        compiler_params=params(8),
    )(live_aux, *(stays(x) for x in (trial_vectors, pair, cond, energy_val)))
    arrived = exchange(sent, ALL)
    sent = direct_call(True, live_aux, arrived, coef_occ, virt, trial, gap)
    arrived = exchange(sent, ALL)
    sent, correction, meet = pl.pallas_call(
        middle_kernel,
        in_specs=[VMEM] * 4,
        out_specs=[VMEM] * 3,
        out_shape=[
            jax.ShapeDtypeStruct((AUX, 8, CB + 128), BF16),
            jax.ShapeDtypeStruct((16, CB), F32),
            jax.ShapeDtypeStruct((K, 128), F32),
        ],
        compiler_params=params(8),
    )(arrived, pair, trial, gap)
    arrived = exchange(sent, SAME_TR)
    sent = direct_call(False, live_aux, arrived, coef_occ, virt)
    arrived = exchange(sent, ALL)
    mine = pl.pallas_call(
        last_kernel,
        in_specs=[VMEM] * 5,
        out_specs=VMEM,
        out_shape=jax.ShapeDtypeStruct((8, 2 * CB + 128), F32),
        compiler_params=params(8),
    )(arrived, pair, correction, gap, meet)
    both = lax.all_gather(mine, "grp")
    applied, intersection = pl.pallas_call(
        join_kernel,
        in_specs=[VMEM],
        out_specs=[VMEM] * 2,
        out_shape=[jax.ShapeDtypeStruct((2, K, CB), F32), jax.ShapeDtypeStruct((K, K), F32)],
        compiler_params=params(4),
    )(both)
    return (applied, intersection)


def solution(mesh):
    mesh = Mesh(mesh.devices.reshape(2, 4, 2, 4, TR), ("grp", "y", "zh", "x", "tr"))
    aux = ("y", "zh", "x")
    in_specs = (
        P(aux, None, "tr"),
        P(aux),
        P("tr"),
        P(aux, None, None),
        P(aux, "tr", None),
        P(aux, "tr", None),
        P(aux),
    )
    out_specs = (P(aux, None, "tr"), P())
    return jax.shard_map(body, mesh=mesh, in_specs=in_specs, out_specs=out_specs, check_vma=False)
```

time: 96.4 us -> 97 us (level)
  Pallas kernels: 18.5 us -> 23.3 us
  blocking collectives: 74.7 us -> 72.1 us
  local copies, waits for them, and re-layouts: 1.49 us -> 0.02 us
    all_gather x1, blocking collectives: 7.72 us -> 1.83 us  [body(): both = lax.all_gather(mine, 'grp')]
    pallas_call x2, Pallas kernels: 14.6 us -> 18.6 us  [direct_call(): pl.pallas_call(functools.partial(direct_kernel, first), in_specs=[SMEM] +...]
    all_to_all x4, blocking collectives: 67 us -> 70.3 us  [exchange(): return lax.all_to_all(x, axes, split_axis=0, concat_axis=0, tiled=True)]
where the time goes in v4:
time: 97 us; the launch traced here: 96.8 us
  blocking collectives  72.1 us (74%)
  Pallas kernels  23.3 us (24%)
  between operations  1.37 us (1%)
    all_to_all x4, blocking collectives, exchange(): return lax.all_to_all(x, axes, split_axis=0, concat_axis=0, tiled=True)  70.3 us
    pallas_call x2, Pallas kernels, direct_call(): pl.pallas_call(functools.partial(direct_kernel, first), in_specs=[SMEM] +...  18.6 us
    pallas_call x1, Pallas kernels, body(): pl.pallas_call(first_kernel, in_specs=[SMEM] + [HBM] * 4, out_specs=[VMEM...  2.05 us

profile of v4, /device:TPU:1, one launch (start us, length us, event | category | flops | bytes accessed | tf_op | source)
XLA Modules:
  0.0 96.8 jit_solution(8222333253270102983)
XLA Ops:
  1.3 0.0 slice-start
  1.3 0.0 slice-start.1
  1.3 0.0 slice-start.2
  1.3 0.0 slice-start.3
  1.3 0.0 copy-start
  1.3 2.0 %shard_map.86 = (bf16[64,8,640]{2,1,0:T(8,128)(2,1)S(1)}, f32[2,8,256]{2,1,0:T(8,128)S(1)}, f32[8,256]{1,0:T(8,128)S(1)}, bf16[512,2048]{1,0:T(8,128)(2,1)S(1)}) custom-call(s32[1]{0:T(128)S(6)} %copy.9.live_ref.refs_0_, f32[2,8,256]{2,1,0:T(8,128)} %trial_hbm.1, bf16[512,2048]{1,0:T(8,128)(2,1)} %bitcast.9, f32[1,256]{1,0:T(1,128)} %bitcast.10, f32[2]{0:T(128)} %val_hbm.1), custom_call_target="tpu_custom_call" | custom-call | flops 20000000000 | bytes 2097152 | tf_op jit(solution)/shard_map/pallas_call | solution.py:366
  3.4 25.6 %all_to_all.20.refs_1_ = bf16[64,8,640]{2,1,0:T(8,128)(2,1)S(1)} all-to-all(bf16[64,8,640]{2,1,0:T(8,128)(2,1)S(1)} %get-tuple-element.9), channel_id=1, replica_groups=mesh['grp'=2,'y'=4,'zh'=2,'x'=4,'tr'=2] {'zh','tr','y','x'}, dimensions={0} | all-to-all | bytes 1310720 | tf_op jit(solution)/shard_map/all_to_all | solution.py:364
  29.0 0.0 slice-done
  29.0 0.0 slice-done.1
  29.0 0.0 slice-done.2
  29.0 0.0 slice-done.3
  29.0 0.0 copy-done
  29.0 9.6 %shard_map.87 = bf16[64,8,384]{2,1,0:T(8,128)(2,1)S(1)} custom-call(s32[1]{0:T(128)S(6)} %copy.9.live_ref.refs_0_, bf16[64,8,640]{2,1,0:T(8,128)(2,1)S(1)} %all_to_all.20.refs_1_, bf16[64,64,64]{2,1,0:T(8,128)(2,1)S(1)} %copy-done, bf16[16384,512]{1,0:T(8,128)(2,1)S(1)} %bitcast.6, f32[2,8,256]{2,1,0:T(8,128)S(1)} %get-tuple-element.10.refs_4_.trial_ref, ...), custom_call_target="tpu_custom_call" | custom-call | tf_op jit(solution)/shard_map/pallas_call | solution.py:348
  38.6 16.2 %all_to_all.21.arrived_ref = bf16[64,8,384]{2,1,0:T(8,128)(2,1)S(1)} all-to-all(bf16[64,8,384]{2,1,0:T(8,128)(2,1)S(1)} %shard_map.87), channel_id=1, replica_groups=mesh['grp'=2,'y'=4,'zh'=2,'x'=4,'tr'=2] {'zh','tr','y','x'}, dimensions={0} | all-to-all | bytes 786432 | tf_op jit(solution)/shard_map/all_to_all | solution.py:364
  54.8 1.3 %shard_map.88 = (bf16[32,8,384]{2,1,0:T(8,128)(2,1)S(1)}, f32[16,256]{1,0:T(8,128)S(1)}, f32[8,128]{1,0:T(8,128)S(1)}) custom-call(bf16[64,8,384]{2,1,0:T(8,128)(2,1)S(1)} %all_to_all.21.arrived_ref, bf16[512,2048]{1,0:T(8,128)(2,1)S(1)} %get-tuple-element.12.pair_ref, f32[2,8,256]{2,1,0:T(8,128)S(1)} %get-tuple-element.10.refs_4_.trial_ref, ...), custom_call_target="tpu_custom_call" | custom-call | tf_op jit(solution)/shard_map/pallas_call | solution.py:387
  56.1 12.9 %all_to_all.22.refs_1_ = bf16[32,8,384]{2,1,0:T(8,128)(2,1)S(1)} all-to-all(bf16[32,8,384]{2,1,0:T(8,128)(2,1)S(1)} %get-tuple-element.13), channel_id=1, replica_groups=mesh['grp'=2,'y'=4,'zh'=2,'x'=4,'tr'=2] {'zh','y','x'}, dimensions={0} | all-to-all | bytes 393216 | tf_op jit(solution)/shard_map/all_to_all | solution.py:364
  68.9 9.1 %shard_map.89 = bf16[64,8,384]{2,1,0:T(8,128)(2,1)S(1)} custom-call(s32[1]{0:T(128)S(6)} %copy.9.live_ref.refs_0_, bf16[32,8,384]{2,1,0:T(8,128)(2,1)S(1)} %all_to_all.22.refs_1_, bf16[64,64,64]{2,1,0:T(8,128)(2,1)S(1)} %copy-done, bf16[16384,512]{1,0:T(8,128)(2,1)S(1)} %bitcast.7), custom_call_target="tpu_custom_call" | custom-call | tf_op jit(solution)/shard_map/pallas_call | solution.py:348
  78.0 15.6 %all_to_all.23.arrived_ref = bf16[64,8,384]{2,1,0:T(8,128)(2,1)S(1)} all-to-all(bf16[64,8,384]{2,1,0:T(8,128)(2,1)S(1)} %shard_map.89), channel_id=1, replica_groups=mesh['grp'=2,'y'=4,'zh'=2,'x'=4,'tr'=2] {'zh','tr','y','x'}, dimensions={0} | all-to-all | bytes 786432 | tf_op jit(solution)/shard_map/all_to_all | solution.py:364
  93.6 0.7 shard_map.90
  94.3 1.8 %all-gather = f32[16,640]{1,0:T(8,128)S(1)} all-gather(f32[8,640]{1,0:T(8,128)S(1)} %shard_map.90), channel_id=2, replica_groups=mesh['grp'=2,'y'=4,'zh'=2,'x'=4,'tr'=2] {'grp'}, dimensions={0}, use_global_device_ids=true | all-gather | bytes 61440 | tf_op jit(solution)/shard_map/all_gather | solution.py:408
  96.1 0.7 shard_map.91
  (1 shorter events, 0.0 us)
Async XLA Ops:
  1.3 27.7 %slice-start = ((s8[16777216]{0:T(1024)(128)(4,1)}), s8[4194304]{0:T(1024)(128)(4,1)S(1)}, s32[]{:S(2)}) async-start(s8[16777216]{0:T(1024)(128)(4,1)} %bitcast.4), calls=%async_computation.4 | async-start | bytes 8388608
  1.3 27.7 %slice-start.1 = ((s8[16777216]{0:T(1024)(128)(4,1)}), s8[4194304]{0:T(1024)(128)(4,1)S(1)}, s32[]{:S(2)}) async-start(s8[16777216]{0:T(1024)(128)(4,1)} %bitcast.4), calls=%async_computation.5 | async-start | bytes 8388608
  1.3 27.7 %slice-start.2 = ((s8[16777216]{0:T(1024)(128)(4,1)}), s8[4194304]{0:T(1024)(128)(4,1)S(1)}, s32[]{:S(2)}) async-start(s8[16777216]{0:T(1024)(128)(4,1)} %bitcast.4), calls=%async_computation.6 | async-start | bytes 8388608
  1.3 27.7 %slice-start.3 = ((s8[16777216]{0:T(1024)(128)(4,1)}), s8[4194304]{0:T(1024)(128)(4,1)S(1)}, s32[]{:S(2)}) async-start(s8[16777216]{0:T(1024)(128)(4,1)} %bitcast.4), calls=%async_computation.7 | async-start | bytes 8388608
  1.3 27.7 %copy-start = (bf16[64,64,64]{2,1,0:T(8,128)(2,1)S(1)}, bf16[64,64,64]{2,1,0:T(8,128)(2,1)}, u32[]{:S(2)}) copy-start(bf16[64,64,64]{2,1,0:T(8,128)(2,1)} %refs_2_.3) | copy-start | bytes 1572868

commit v5 on v3

--- a/solution.py
+++ b/solution.py
@@ -5,6 +5,7 @@
 from jax import lax
 from jax.experimental import pallas as pl
 from jax.experimental.pallas import tpu as pltpu
+from jax.sharding import Mesh
 from jax.sharding import PartitionSpec as P
 
 V = 64
@@ -15,6 +16,8 @@
 TR = 2
 CB = C // TR
 PAIRS = AUX * TR
+ALL = ("zh", "tr", "y", "x")
+SAME_TR = ("zh", "y", "x")
 SLOTS = 64
 NAUX = 2048
 BLOCK = 8
@@ -30,6 +33,16 @@
 NT = (((1,), (1,)), ((), ()))
 
 
+def place(a, t):
+    y, zh, x = a // 8, a // 4 % 2, a % 4
+    return zh * 32 + t * 16 + y * 4 + x
+
+
+def place_same_tr(a):
+    y, zh, x = a // 8, a // 4 % 2, a % 4
+    return zh * 16 + y * 4 + x
+
+
 def stays(x):
     return pltpu.with_memory_space_constraint(x, pltpu.HBM)
 
@@ -57,14 +70,14 @@
 def first_kernel(
     live_ref, trial_hbm, pair_hbm, cond_hbm, val_hbm, out_ref, trial_ref, gap_ref, pair_ref, cond_ref, val_ref, sems
 ):
-    parts = [pl.ds(NAUX // PARTS * i, NAUX // PARTS) for i in range(PARTS)]
+    parts = [pl.ds(2 * CB // PARTS * i, 2 * CB // PARTS) for i in range(PARTS)]
     copies = [
         pltpu.make_async_copy(trial_hbm, trial_ref, sems.at[0]),
         pltpu.make_async_copy(cond_hbm, cond_ref, sems.at[1]),
         pltpu.make_async_copy(val_hbm, val_ref, sems.at[2]),
     ]
     for i in range(PARTS):
-        copies.append(pltpu.make_async_copy(pair_hbm.at[:, parts[i]], pair_ref.at[:, parts[i]], sems.at[3 + i]))
+        copies.append(pltpu.make_async_copy(pair_hbm.at[parts[i]], pair_ref.at[parts[i]], sems.at[3 + i]))
     for copy in copies:
         copy.start()
     copies[0].wait()
@@ -75,13 +88,15 @@
     copies[2].wait()
     for v in range(2):
         gap_ref[HALF * v : HALF * v + HALF] = jnp.broadcast_to(cond_ref[...] - val_ref[v], (HALF, CB))
+    projection = jnp.zeros((K, NAUX), F32)
     for i in range(PARTS):
         copies[3 + i].wait()
-        projection = dot(wide, pair_ref[:, parts[i]]).astype(BF16)
-        for tile in range(TILES // PARTS):
-            for device in range(4):
-                at = 4 * (TILES // PARTS * i + tile) + device
-                out_ref[at, :, 2 * CB :] = projection[:, 128 * tile : 128 * tile + 128]
+        rows = slice(2 * CB // PARTS * i, 2 * CB // PARTS * (i + 1))
+        projection += dot(wide[:, rows], pair_ref[rows])
+    projection = projection.astype(BF16)
+    for device in range(PAIRS):
+        tile = device // 4
+        out_ref[device, :, 2 * CB :] = projection[:, 128 * tile : 128 * tile + 128]
 
 
 def direct_kernel(first, *refs):
@@ -91,13 +106,13 @@
     else:
         live_ref, arrived_ref, occ_ref, virt_ref = refs[:4]
         out_ref, vectors_ref, blended_ref, total_ref = refs[4:]
-    core, aux, tr = lax.axis_index("grp"), lax.axis_index("aux"), lax.axis_index("tr")
+    core, tr, quarter = lax.axis_index("grp"), lax.axis_index("tr"), lax.axis_index("x")
 
     row = lax.broadcasted_iota(jnp.int32, (HALF * V, 1), 0)
     if first:
         for a in range(AUX):
             for t in range(TR):
-                slab = arrived_ref[2 * a + t, :, : 2 * CB].astype(F32)
+                slab = arrived_ref[place(a, t), :, : 2 * CB].astype(F32)
                 rows_ref[t, 16 * a : 16 * a + 16] = both_halves(slab).astype(BF16)
         chosen = lax.broadcasted_iota(jnp.int32, (HALF * V, K * V), 1)
         wanted = K * (row % V) + HALF * core + row // V
@@ -105,7 +120,8 @@
     else:
         chosen = lax.broadcasted_iota(jnp.int32, (HALF * V, HALF * V), 1)
         wanted = HALF * (row % V) + row // V
-        wide = arrived_ref[:, :, :CB].astype(F32).reshape(HALF * V, CB).astype(BF16)
+        wide = [arrived_ref[place_same_tr(a), :, :CB].astype(F32) for a in range(AUX)]
+        wide = jnp.concatenate(wide, axis=0).astype(BF16)
     vectors_ref[...] = dot((chosen == wanted).astype(BF16), wide).astype(BF16)
 
     live = live_ref[0]
@@ -157,7 +173,6 @@
         projection = jnp.zeros((K, 128), F32)
         for device in range(PAIRS):
             projection += arrived_ref[device, :, 2 * CB :].astype(F32)
-        quarter = (TR * aux + tr) % 4
         extra = jnp.where(lanes // 32 == quarter, projection, kept)
     else:
         extra = jnp.zeros((K, 128), F32)
@@ -166,8 +181,8 @@
     extra = extra.astype(BF16)
     for a in range(AUX):
         for t in range(TR):
-            out_ref[2 * a + t, :, :CB] = owned[8 * a : 8 * a + 8, CB * t : CB * t + CB].astype(BF16)
-            out_ref[2 * a + t, :, CB:] = extra
+            out_ref[place(a, t), :, :CB] = owned[8 * a : 8 * a + 8, CB * t : CB * t + CB].astype(BF16)
+            out_ref[place(a, t), :, CB:] = extra
 
 
 def direct_sum(arrived_ref):
@@ -230,16 +245,26 @@
         out_ref[a, :, CB:] = projection[:, 128 * tile : 128 * tile + 128]
 
 
-def last_kernel(arrived_ref, pair_ref, correction_ref, gap_ref, out_ref):
+def last_kernel(arrived_ref, pair_ref, correction_ref, gap_ref, meet_ref, out_ref):
     direct = direct_sum(arrived_ref)
     tiles = []
     for tile in range(TILES):
-        whole = arrived_ref[4 * tile, :, CB:].astype(F32) + arrived_ref[4 * tile + 1, :, CB:].astype(F32)
+        at = tile // 8 * 32 + 2 * tile % 16
+        whole = arrived_ref[at, :, CB:].astype(F32) + arrived_ref[at + 16, :, CB:].astype(F32)
         tiles.append(whole.astype(BF16))
     projection = jnp.concatenate(tiles, axis=1)
     exchange = lax.dot_general(projection, pair_ref[...], NT, preferred_element_type=F32)
     exchange = jnp.concatenate([exchange[:HALF, :CB], exchange[:HALF, CB:]], axis=0)
-    out_ref[...] = gap_ref[...] * correction_ref[...] + direct + exchange
+    out_ref[:, :CB] = gap_ref[...] * correction_ref[...] + direct + exchange
+    out_ref[:, CB:] = meet_ref[...]
+
+
+def join_kernel(both_ref, applied_ref, meet_ref):
+    for v in range(2):
+        rows = [both_ref[core, HALF * v : HALF * v + HALF, :CB] for core in range(2)]
+        applied_ref[v] = jnp.concatenate(rows, axis=0)
+    columns = [both_ref[core, :, CB : CB + HALF] for core in range(2)]
+    meet_ref[...] = jnp.concatenate(columns, axis=1)
 
 
 def direct_call(first, live, arrived, occ, virt, *local):
@@ -287,9 +312,9 @@
         cost_estimate=pl.CostEstimate(flops=UNTIL_DIRECT, bytes_accessed=2 * pair.size, transcendentals=0),
         compiler_params=params(8),
     )(live_aux, *(stays(x) for x in (trial_vectors, pair, cond, energy_val)))
-    arrived = exchange(sent, ("aux", "tr"))
+    arrived = exchange(sent, ALL)
     sent = direct_call(True, live_aux, arrived, coef_occ, virt, trial, gap)
-    arrived = exchange(sent, ("aux", "tr"))
+    arrived = exchange(sent, ALL)
     sent, correction, meet = pl.pallas_call(
         middle_kernel,
         in_specs=[VMEM] * 4,
@@ -301,31 +326,38 @@
         ],
         compiler_params=params(8),
     )(arrived, pair, trial, gap)
-    arrived = exchange(sent, ("aux",))
+    arrived = exchange(sent, SAME_TR)
     sent = direct_call(False, live_aux, arrived, coef_occ, virt)
-    arrived = exchange(sent, ("aux", "tr"))
-    applied = pl.pallas_call(
+    arrived = exchange(sent, ALL)
+    mine = pl.pallas_call(
         last_kernel,
-        in_specs=[VMEM] * 4,
+        in_specs=[VMEM] * 5,
         out_specs=VMEM,
-        out_shape=jax.ShapeDtypeStruct((2 * HALF, CB), F32),
+        out_shape=jax.ShapeDtypeStruct((2 * HALF, CB + 128), F32),
         compiler_params=params(8),
-    )(arrived, pair, correction, gap)
-    both = lax.all_gather(jnp.concatenate([applied, meet], axis=1), "grp")
-    applied = both[:, :, :CB].reshape(2, 2, HALF, CB).transpose(1, 0, 2, 3).reshape(2, K, CB)
-    intersection = jnp.concatenate([both[0, :, CB : CB + HALF], both[1, :, CB : CB + HALF]], axis=1)
+    )(arrived, pair, correction, gap, meet)
+    both = lax.all_gather(mine, "grp")
+    applied, intersection = pl.pallas_call(
+        join_kernel,
+        in_specs=[VMEM],
+        out_specs=[VMEM] * 2,
+        out_shape=[jax.ShapeDtypeStruct((2, K, CB), F32), jax.ShapeDtypeStruct((K, K), F32)],
+        compiler_params=params(4),
+    )(both)
     return (applied, intersection)
 
 
 def solution(mesh):
+    mesh = Mesh(mesh.devices.reshape(2, 4, 2, 4, TR), ("grp", "y", "zh", "x", "tr"))
+    aux = ("y", "zh", "x")
     in_specs = (
-        P("aux", None, "tr"),
-        P("aux"),
+        P(aux, None, "tr"),
+        P(aux),
         P("tr"),
-        P("aux", None, None),
-        P("aux", "tr", None),
-        P("aux", "tr", None),
-        P("aux"),
+        P(aux, None, None),
+        P(aux, "tr", None),
+        P(aux, "tr", None),
+        P(aux),
     )
-    out_specs = (P("aux", None, "tr"), P())
+    out_specs = (P(aux, None, "tr"), P())
     return jax.shard_map(body, mesh=mesh, in_specs=in_specs, out_specs=out_specs, check_vma=False)

time: 96.4 us -> 95.5 us (level)
  local copies, waits for them, and re-layouts: 1.49 us -> 0.02 us
where the time goes in v5:
time: 95.5 us; the launch traced here: 95.3 us
  blocking collectives  74.8 us (78%)
  Pallas kernels  19 us (20%)
  between operations  1.37 us (1%)
    all_to_all x4, blocking collectives, exchange(): return lax.all_to_all(x, axes, split_axis=0, concat_axis=0, tiled=True)  67.3 us
    pallas_call x2, Pallas kernels, direct_call(): pl.pallas_call(functools.partial(direct_kernel, first), in_specs=[SMEM] +...  14.6 us
    all_gather x1, blocking collectives, body(): both = lax.all_gather(mine, 'grp')  7.52 us
    pallas_call x1, Pallas kernels, body(): pl.pallas_call(first_kernel, in_specs=[SMEM] + [HBM] * 4, out_specs=[VMEM...  1.95 us

profile of v5, /device:TPU:1, one launch (start us, length us, event | category | flops | bytes accessed | tf_op | source)
XLA Modules:
  0.0 95.3 jit_solution(9087060957437007441)
XLA Ops:
  1.3 0.0 slice-start
  1.3 0.0 slice-start.1
  1.3 0.0 slice-start.2
  1.3 0.0 slice-start.3
  1.3 0.0 copy-start
  1.3 1.9 %shard_map.86 = (bf16[64,8,640]{2,1,0:T(8,128)(2,1)S(1)}, f32[2,8,256]{2,1,0:T(8,128)S(1)}, f32[8,256]{1,0:T(8,128)S(1)}, bf16[512,2048]{1,0:T(8,128)(2,1)S(1)}) custom-call(s32[1]{0:T(128)S(6)} %copy.9.live_ref.refs_0_, f32[2,8,256]{2,1,0:T(8,128)} %trial_hbm.1, bf16[512,2048]{1,0:T(8,128)(2,1)} %bitcast.9, f32[1,256]{1,0:T(1,128)} %bitcast.10, f32[2]{0:T(128)} %val_hbm.1), custom_call_target="tpu_custom_call" | custom-call | flops 20000000000 | bytes 2097152 | tf_op jit(solution)/shard_map/pallas_call | solution.py:297
  3.3 25.6 %all_to_all.20.refs_1_ = bf16[64,8,640]{2,1,0:T(8,128)(2,1)S(1)} all-to-all(bf16[64,8,640]{2,1,0:T(8,128)(2,1)S(1)} %get-tuple-element.9), channel_id=1, replica_groups=mesh['grp'=2,'y'=4,'zh'=2,'x'=4,'tr'=2] {'zh','tr','y','x'}, dimensions={0} | all-to-all | bytes 1310720 | tf_op jit(solution)/shard_map/all_to_all | solution.py:295
  28.9 0.0 slice-done
  28.9 0.0 slice-done.1
  28.9 0.0 slice-done.2
  28.9 0.0 slice-done.3
  28.9 0.0 copy-done
  28.9 7.5 %shard_map.87 = bf16[64,8,384]{2,1,0:T(8,128)(2,1)S(1)} custom-call(s32[1]{0:T(128)S(6)} %copy.9.live_ref.refs_0_, bf16[64,8,640]{2,1,0:T(8,128)(2,1)S(1)} %all_to_all.20.refs_1_, bf16[64,64,64]{2,1,0:T(8,128)(2,1)S(1)} %copy-done, bf16[16384,512]{1,0:T(8,128)(2,1)S(1)} %bitcast.6, f32[2,8,256]{2,1,0:T(8,128)S(1)} %get-tuple-element.10.refs_4_.trial_ref, ...), custom_call_target="tpu_custom_call" | custom-call | tf_op jit(solution)/shard_map/pallas_call | solution.py:279
  36.4 14.5 %all_to_all.21.arrived_ref = bf16[64,8,384]{2,1,0:T(8,128)(2,1)S(1)} all-to-all(bf16[64,8,384]{2,1,0:T(8,128)(2,1)S(1)} %shard_map.87), channel_id=1, replica_groups=mesh['grp'=2,'y'=4,'zh'=2,'x'=4,'tr'=2] {'zh','tr','y','x'}, dimensions={0} | all-to-all | bytes 786432 | tf_op jit(solution)/shard_map/all_to_all | solution.py:295
  50.9 1.2 %shard_map.88 = (bf16[32,8,384]{2,1,0:T(8,128)(2,1)S(1)}, f32[8,256]{1,0:T(8,128)S(1)}, f32[8,128]{1,0:T(8,128)S(1)}) custom-call(bf16[64,8,384]{2,1,0:T(8,128)(2,1)S(1)} %all_to_all.21.arrived_ref, bf16[512,2048]{1,0:T(8,128)(2,1)S(1)} %get-tuple-element.12.pair_ref, f32[2,8,256]{2,1,0:T(8,128)S(1)} %get-tuple-element.10.refs_4_.trial_ref, ...), custom_call_target="tpu_custom_call" | custom-call | tf_op jit(solution)/shard_map/pallas_call | solution.py:318
  52.1 13.0 %all_to_all.22.refs_1_ = bf16[32,8,384]{2,1,0:T(8,128)(2,1)S(1)} all-to-all(bf16[32,8,384]{2,1,0:T(8,128)(2,1)S(1)} %get-tuple-element.13), channel_id=1, replica_groups=mesh['grp'=2,'y'=4,'zh'=2,'x'=4,'tr'=2] {'zh','y','x'}, dimensions={0} | all-to-all | bytes 393216 | tf_op jit(solution)/shard_map/all_to_all | solution.py:295
  65.1 7.0 %shard_map.89 = bf16[64,8,384]{2,1,0:T(8,128)(2,1)S(1)} custom-call(s32[1]{0:T(128)S(6)} %copy.9.live_ref.refs_0_, bf16[32,8,384]{2,1,0:T(8,128)(2,1)S(1)} %all_to_all.22.refs_1_, bf16[64,64,64]{2,1,0:T(8,128)(2,1)S(1)} %copy-done, bf16[16384,512]{1,0:T(8,128)(2,1)S(1)} %bitcast.7), custom_call_target="tpu_custom_call" | custom-call | tf_op jit(solution)/shard_map/pallas_call | solution.py:279
  72.2 14.3 %all_to_all.23.arrived_ref = bf16[64,8,384]{2,1,0:T(8,128)(2,1)S(1)} all-to-all(bf16[64,8,384]{2,1,0:T(8,128)(2,1)S(1)} %shard_map.89), channel_id=1, replica_groups=mesh['grp'=2,'y'=4,'zh'=2,'x'=4,'tr'=2] {'zh','tr','y','x'}, dimensions={0} | all-to-all | bytes 786432 | tf_op jit(solution)/shard_map/all_to_all | solution.py:295
  86.4 0.7 shard_map.90
  87.1 7.5 %all-gather = f32[16,384]{1,0:T(8,128)S(1)} all-gather(f32[8,384]{1,0:T(8,128)S(1)} %shard_map.90), channel_id=2, replica_groups=mesh['grp'=2,'y'=4,'zh'=2,'x'=4,'tr'=2] {'grp'}, dimensions={0}, use_global_device_ids=true | all-gather | bytes 36864 | tf_op jit(solution)/shard_map/all_gather | solution.py:339
  94.6 0.7 shard_map.91
  (1 shorter events, 0.0 us)
Async XLA Ops:
  1.3 27.6 %slice-start = ((s8[16777216]{0:T(1024)(128)(4,1)}), s8[4194304]{0:T(1024)(128)(4,1)S(1)}, s32[]{:S(2)}) async-start(s8[16777216]{0:T(1024)(128)(4,1)} %bitcast.4), calls=%async_computation.4 | async-start | bytes 8388608
  1.3 27.6 %slice-start.1 = ((s8[16777216]{0:T(1024)(128)(4,1)}), s8[4194304]{0:T(1024)(128)(4,1)S(1)}, s32[]{:S(2)}) async-start(s8[16777216]{0:T(1024)(128)(4,1)} %bitcast.4), calls=%async_computation.5 | async-start | bytes 8388608
  1.3 27.6 %slice-start.2 = ((s8[16777216]{0:T(1024)(128)(4,1)}), s8[4194304]{0:T(1024)(128)(4,1)S(1)}, s32[]{:S(2)}) async-start(s8[16777216]{0:T(1024)(128)(4,1)} %bitcast.4), calls=%async_computation.6 | async-start | bytes 8388608
  1.3 27.6 %slice-start.3 = ((s8[16777216]{0:T(1024)(128)(4,1)}), s8[4194304]{0:T(1024)(128)(4,1)S(1)}, s32[]{:S(2)}) async-start(s8[16777216]{0:T(1024)(128)(4,1)} %bitcast.4), calls=%async_computation.7 | async-start | bytes 8388608
  1.3 27.6 %copy-start = (bf16[64,64,64]{2,1,0:T(8,128)(2,1)S(1)}, bf16[64,64,64]{2,1,0:T(8,128)(2,1)}, u32[]{:S(2)}) copy-start(bf16[64,64,64]{2,1,0:T(8,128)(2,1)} %refs_2_.3) | copy-start | bytes 1572868

commit v6 on v5

--- a/solution.py
+++ b/solution.py
@@ -119,8 +119,9 @@
         wide = rows_ref[tr]
     else:
         chosen = lax.broadcasted_iota(jnp.int32, (HALF * V, HALF * V), 1)
-        wanted = HALF * (row % V) + row // V
-        wide = [arrived_ref[place_same_tr(a), :, :CB].astype(F32) for a in range(AUX)]
+        wanted = HALF * AUX * (row % 2) + HALF * (row % V // 2) + row // V
+        slabs = [arrived_ref[place_same_tr(a)].astype(F32) for a in range(AUX)]
+        wide = [slabs[a][:, CB * u : CB * u + CB] for u in range(2) for a in range(AUX)]
         wide = jnp.concatenate(wide, axis=0).astype(BF16)
     vectors_ref[...] = dot((chosen == wanted).astype(BF16), wide).astype(BF16)
 
@@ -148,8 +149,12 @@
 
     lanes = lane_ids((K, 128))
     total = total_ref[...].astype(BF16)
-    chosen = lax.broadcasted_iota(jnp.int32, (HALF * V, HALF * V), 1)
-    owned = dot((chosen == V * (row % HALF) + row // HALF).astype(BF16), total).astype(BF16).astype(F32)
+    row = lax.broadcasted_iota(jnp.int32, (HALF * AUX, 1), 0)
+    chosen = lax.broadcasted_iota(jnp.int32, (HALF * AUX, HALF * V), 1)
+    owned = []
+    for u in range(2):
+        taken = chosen == V * (row % HALF) + 2 * (row // HALF) + u
+        owned.append(dot(taken.astype(BF16), total).astype(BF16).astype(F32))
     if first:
         shares = jnp.zeros((K, HALF * V), F32)
         for t in range(TR):
@@ -174,22 +179,26 @@
         for device in range(PAIRS):
             projection += arrived_ref[device, :, 2 * CB :].astype(F32)
         extra = jnp.where(lanes // 32 == quarter, projection, kept)
+        near = lax.rem(lanes // 32 - quarter + 4, 4) < 2
+        extra = jnp.where(near, extra, pltpu.roll(pltpu.roll(extra, 64, 1), 4, 0))[:HALF]
     else:
-        extra = jnp.zeros((K, 128), F32)
-        for a in range(AUX):
-            extra += arrived_ref[a, :, CB:].astype(F32)
+        extra = jnp.zeros((HALF, 128), F32)
+        for slab in slabs:
+            extra += slab[:, 2 * CB :]
     extra = extra.astype(BF16)
     for a in range(AUX):
         for t in range(TR):
-            out_ref[place(a, t), :, :CB] = owned[8 * a : 8 * a + 8, CB * t : CB * t + CB].astype(BF16)
-            out_ref[place(a, t), :, CB:] = extra
+            for u in range(2):
+                part = owned[u][HALF * a : HALF * a + HALF, CB * t : CB * t + CB]
+                out_ref[place(a, t), :, CB * u : CB * u + CB] = part.astype(BF16)
+            out_ref[place(a, t), :, 2 * CB :] = extra
 
 
 def direct_sum(arrived_ref):
-    total = jnp.zeros((2 * HALF, CB), F32)
+    total = jnp.zeros((HALF, 2 * CB), F32)
     for device in range(PAIRS):
-        total += arrived_ref[device, :, :CB].astype(F32)
-    return total
+        total += arrived_ref[device, :, : 2 * CB].astype(F32)
+    return jnp.concatenate([total[:, :CB], total[:, CB:]], axis=0)
 
 
 def middle_kernel(
@@ -197,23 +206,29 @@
 ):
     core = lax.axis_index("grp")
     direct = direct_sum(arrived_ref)
-    lanes = lane_ids((K, 128))
+    few, lanes = lane_ids((HALF, 128)), lane_ids((K, 128))
+    upper = lax.broadcasted_iota(jnp.int32, (K, 128), 0) < HALF
     tiles = []
-    sums = [jnp.zeros((K, 128), F32) for _ in range(4)]
+    sums = [jnp.zeros((HALF, 128), F32) for _ in range(4)]
     for tile in range(TILES):
-        whole = jnp.zeros((K, 128), F32)
+        low = high = jnp.zeros((HALF, 128), F32)
         for quarter in range(4):
-            extra = arrived_ref[4 * tile + quarter, :, CB:].astype(F32)
-            whole = jnp.where(lanes // 32 == quarter, extra, whole)
+            extra = arrived_ref[4 * tile + quarter, :, 2 * CB :].astype(F32)
+            low = jnp.where(few // 32 == quarter, extra, low)
+            high = jnp.where(few // 32 == (quarter + 2) % 4, extra, high)
             sums[quarter] += extra
+        whole = jnp.concatenate([low, high], axis=0)
+        whole = jnp.where(upper, whole, pltpu.roll(whole, 64, 1))
         tiles.append(whole.astype(BF16))
     projection = jnp.concatenate(tiles, axis=1)
     exchange_full = lax.dot_general(projection, pair_ref[...], NT, preferred_element_type=F32)
     mine = own_rows(core, exchange_full)
     exchange = jnp.concatenate([mine[:, :CB], mine[:, CB:]], axis=0)
-    shares = jnp.zeros((K, 128), F32)
+    low = high = jnp.zeros((HALF, 128), F32)
     for quarter in range(4):
-        shares += jnp.where(lanes // 32 == (quarter + 1) % 4, sums[quarter], 0.0)
+        low = jnp.where(few // 32 == (quarter + 1) % 4, sums[quarter], low)
+        high = jnp.where(few // 32 == (quarter + 3) % 4, sums[quarter], high)
+    shares = jnp.concatenate([low, high], axis=0)
     meet_exchange = lax.dot_general(projection, projection, NT, preferred_element_type=F32)
     meet = []
     for j in range(HALF):
@@ -235,14 +250,14 @@
     )
     correction = (applied - overlap) / gap
     correction_ref[...] = correction
-    rounded = correction.astype(BF16)
-    wide = jnp.concatenate([correction[:HALF], correction[HALF:]], axis=1)
-    wide = jnp.concatenate([wide, jnp.zeros_like(wide)], axis=0).astype(BF16)
-    projection = dot(wide, pair_ref[...]).astype(BF16)
+    few = jnp.concatenate([correction[:HALF], correction[HALF:]], axis=1)
+    wide = jnp.concatenate([few, jnp.zeros_like(few)], axis=0).astype(BF16)
+    projection = dot(wide, pair_ref[...])[:HALF].astype(BF16)
+    rounded = few.astype(BF16)
     for a in range(AUX):
         tile = a // 2
-        out_ref[a, :, :CB] = rounded
-        out_ref[a, :, CB:] = projection[:, 128 * tile : 128 * tile + 128]
+        out_ref[a, :, : 2 * CB] = rounded
+        out_ref[a, :, 2 * CB :] = projection[:, 128 * tile : 128 * tile + 128]
 
 
 def last_kernel(arrived_ref, pair_ref, correction_ref, gap_ref, meet_ref, out_ref):
@@ -250,9 +265,9 @@
     tiles = []
     for tile in range(TILES):
         at = tile // 8 * 32 + 2 * tile % 16
-        whole = arrived_ref[at, :, CB:].astype(F32) + arrived_ref[at + 16, :, CB:].astype(F32)
-        tiles.append(whole.astype(BF16))
-    projection = jnp.concatenate(tiles, axis=1)
+        tiles.append(arrived_ref[at, :, 2 * CB :].astype(F32) + arrived_ref[at + 16, :, 2 * CB :].astype(F32))
+    few = jnp.concatenate(tiles, axis=1)
+    projection = jnp.concatenate([few, jnp.zeros_like(few)], axis=0).astype(BF16)
     exchange = lax.dot_general(projection, pair_ref[...], NT, preferred_element_type=F32)
     exchange = jnp.concatenate([exchange[:HALF, :CB], exchange[:HALF, CB:]], axis=0)
     out_ref[:, :CB] = gap_ref[...] * correction_ref[...] + direct + exchange
@@ -268,7 +283,7 @@
 
 
 def direct_call(first, live, arrived, occ, virt, *local):
-    out = jax.ShapeDtypeStruct((PAIRS, 2 * HALF, CB + 128), BF16)
+    out = jax.ShapeDtypeStruct((PAIRS, HALF, 2 * CB + 128), BF16)
     scratch = [
         pltpu.VMEM((HALF * V, CB), BF16),
         pltpu.VMEM((2, HALF * V, BLOCK * CB), BF16),
@@ -320,7 +335,7 @@
         in_specs=[VMEM] * 4,
         out_specs=[VMEM] * 3,
         out_shape=[
-            jax.ShapeDtypeStruct((AUX, 2 * HALF, CB + 128), BF16),
+            jax.ShapeDtypeStruct((AUX, HALF, 2 * CB + 128), BF16),
             jax.ShapeDtypeStruct((2 * HALF, CB), F32),
             jax.ShapeDtypeStruct((K, 128), F32),
         ],

time: 95.5 us -> 94.9 us (level)
  no operation moved by 1% of the time
where the time goes in v6:
time: 94.9 us; the launch traced here: 94.7 us
  blocking collectives  74 us (78%)
  Pallas kernels  19.2 us (20%)
  between operations  1.37 us (1%)
    all_to_all x4, blocking collectives, exchange(): return lax.all_to_all(x, axes, split_axis=0, concat_axis=0, tiled=True)  66.5 us
    pallas_call x2, Pallas kernels, direct_call(): pl.pallas_call(functools.partial(direct_kernel, first), in_specs=[SMEM] +...  14.8 us
    all_gather x1, blocking collectives, body(): both = lax.all_gather(mine, 'grp')  7.55 us
    pallas_call x1, Pallas kernels, body(): pl.pallas_call(first_kernel, in_specs=[SMEM] + [HBM] * 4, out_specs=[VMEM...  1.95 us

profile of v6, /device:TPU:1, one launch (start us, length us, event | category | flops | bytes accessed | tf_op | source)
XLA Modules:
  0.0 94.7 jit_solution(17999426594671486341)
XLA Ops:
  1.3 0.0 slice-start
  1.3 0.0 slice-start.1
  1.3 0.0 slice-start.2
  1.3 0.0 slice-start.3
  1.3 0.0 copy-start
  1.3 1.9 %shard_map.86 = (bf16[64,8,640]{2,1,0:T(8,128)(2,1)S(1)}, f32[2,8,256]{2,1,0:T(8,128)S(1)}, f32[8,256]{1,0:T(8,128)S(1)}, bf16[512,2048]{1,0:T(8,128)(2,1)S(1)}) custom-call(s32[1]{0:T(128)S(6)} %copy.9.live_ref.refs_0_, f32[2,8,256]{2,1,0:T(8,128)} %trial_hbm.1, bf16[512,2048]{1,0:T(8,128)(2,1)} %bitcast.9, f32[1,256]{1,0:T(1,128)} %bitcast.10, f32[2]{0:T(128)} %val_hbm.1), custom_call_target="tpu_custom_call" | custom-call | flops 20000000000 | bytes 2097152 | tf_op jit(solution)/shard_map/pallas_call | solution.py:312
  3.3 25.6 %all_to_all.20.refs_1_ = bf16[64,8,640]{2,1,0:T(8,128)(2,1)S(1)} all-to-all(bf16[64,8,640]{2,1,0:T(8,128)(2,1)S(1)} %get-tuple-element.9), channel_id=1, replica_groups=mesh['grp'=2,'y'=4,'zh'=2,'x'=4,'tr'=2] {'zh','tr','y','x'}, dimensions={0} | all-to-all | bytes 1310720 | tf_op jit(solution)/shard_map/all_to_all | solution.py:310
  28.9 0.0 slice-done
  28.9 0.0 slice-done.1
  28.9 0.0 slice-done.2
  28.9 0.0 slice-done.3
  28.9 0.0 copy-done
  28.9 7.7 %shard_map.87 = bf16[64,4,640]{2,1,0:T(4,128)(2,1)S(1)} custom-call(s32[1]{0:T(128)S(6)} %copy.9.live_ref.refs_0_, bf16[64,8,640]{2,1,0:T(8,128)(2,1)S(1)} %all_to_all.20.refs_1_, bf16[64,64,64]{2,1,0:T(8,128)(2,1)S(1)} %copy-done, bf16[16384,512]{1,0:T(8,128)(2,1)S(1)} %bitcast.6, f32[2,8,256]{2,1,0:T(8,128)S(1)} %get-tuple-element.10.refs_4_.trial_ref, ...), custom_call_target="tpu_custom_call" | custom-call | tf_op jit(solution)/shard_map/pallas_call | solution.py:294
  36.6 14.1 %all_to_all.21.arrived_ref = bf16[64,4,640]{2,1,0:T(4,128)(2,1)S(1)} all-to-all(bf16[64,4,640]{2,1,0:T(4,128)(2,1)S(1)} %shard_map.87), channel_id=1, replica_groups=mesh['grp'=2,'y'=4,'zh'=2,'x'=4,'tr'=2] {'zh','tr','y','x'}, dimensions={0} | all-to-all | bytes 655360 | tf_op jit(solution)/shard_map/all_to_all | solution.py:310
  50.7 1.2 %shard_map.88 = (bf16[32,4,640]{2,1,0:T(4,128)(2,1)S(1)}, f32[8,256]{1,0:T(8,128)S(1)}, f32[8,128]{1,0:T(8,128)S(1)}) custom-call(bf16[64,4,640]{2,1,0:T(4,128)(2,1)S(1)} %all_to_all.21.arrived_ref, bf16[512,2048]{1,0:T(8,128)(2,1)S(1)} %get-tuple-element.12.pair_ref, f32[2,8,256]{2,1,0:T(8,128)S(1)} %get-tuple-element.10.refs_4_.trial_ref, ...), custom_call_target="tpu_custom_call" | custom-call | tf_op jit(solution)/shard_map/pallas_call | solution.py:333
  51.9 12.9 %all_to_all.22.refs_1_ = bf16[32,4,640]{2,1,0:T(4,128)(2,1)S(1)} all-to-all(bf16[32,4,640]{2,1,0:T(4,128)(2,1)S(1)} %get-tuple-element.13), channel_id=1, replica_groups=mesh['grp'=2,'y'=4,'zh'=2,'x'=4,'tr'=2] {'zh','y','x'}, dimensions={0} | all-to-all | bytes 327680 | tf_op jit(solution)/shard_map/all_to_all | solution.py:310
  64.8 7.1 %shard_map.89 = bf16[64,4,640]{2,1,0:T(4,128)(2,1)S(1)} custom-call(s32[1]{0:T(128)S(6)} %copy.9.live_ref.refs_0_, bf16[32,4,640]{2,1,0:T(4,128)(2,1)S(1)} %all_to_all.22.refs_1_, bf16[64,64,64]{2,1,0:T(8,128)(2,1)S(1)} %copy-done, bf16[16384,512]{1,0:T(8,128)(2,1)S(1)} %bitcast.7), custom_call_target="tpu_custom_call" | custom-call | tf_op jit(solution)/shard_map/pallas_call | solution.py:294
  71.9 13.9 %all_to_all.23.arrived_ref = bf16[64,4,640]{2,1,0:T(4,128)(2,1)S(1)} all-to-all(bf16[64,4,640]{2,1,0:T(4,128)(2,1)S(1)} %shard_map.89), channel_id=1, replica_groups=mesh['grp'=2,'y'=4,'zh'=2,'x'=4,'tr'=2] {'zh','tr','y','x'}, dimensions={0} | all-to-all | bytes 655360 | tf_op jit(solution)/shard_map/all_to_all | solution.py:310
  85.8 0.7 shard_map.90
  86.5 7.5 %all-gather = f32[16,384]{1,0:T(8,128)S(1)} all-gather(f32[8,384]{1,0:T(8,128)S(1)} %shard_map.90), channel_id=2, replica_groups=mesh['grp'=2,'y'=4,'zh'=2,'x'=4,'tr'=2] {'grp'}, dimensions={0}, use_global_device_ids=true | all-gather | bytes 36864 | tf_op jit(solution)/shard_map/all_gather | solution.py:354
  94.0 0.7 shard_map.91
  (1 shorter events, 0.0 us)
Async XLA Ops:
  1.3 27.6 %slice-start = ((s8[16777216]{0:T(1024)(128)(4,1)}), s8[4194304]{0:T(1024)(128)(4,1)S(1)}, s32[]{:S(2)}) async-start(s8[16777216]{0:T(1024)(128)(4,1)} %bitcast.4), calls=%async_computation.4 | async-start | bytes 8388608
  1.3 27.6 %slice-start.1 = ((s8[16777216]{0:T(1024)(128)(4,1)}), s8[4194304]{0:T(1024)(128)(4,1)S(1)}, s32[]{:S(2)}) async-start(s8[16777216]{0:T(1024)(128)(4,1)} %bitcast.4), calls=%async_computation.5 | async-start | bytes 8388608
  1.3 27.6 %slice-start.2 = ((s8[16777216]{0:T(1024)(128)(4,1)}), s8[4194304]{0:T(1024)(128)(4,1)S(1)}, s32[]{:S(2)}) async-start(s8[16777216]{0:T(1024)(128)(4,1)} %bitcast.4), calls=%async_computation.6 | async-start | bytes 8388608
  1.3 27.6 %slice-start.3 = ((s8[16777216]{0:T(1024)(128)(4,1)}), s8[4194304]{0:T(1024)(128)(4,1)S(1)}, s32[]{:S(2)}) async-start(s8[16777216]{0:T(1024)(128)(4,1)} %bitcast.4), calls=%async_computation.7 | async-start | bytes 8388608
  1.3 27.6 %copy-start = (bf16[64,64,64]{2,1,0:T(8,128)(2,1)S(1)}, bf16[64,64,64]{2,1,0:T(8,128)(2,1)}, u32[]{:S(2)}) copy-start(bf16[64,64,64]{2,1,0:T(8,128)(2,1)} %refs_2_.3) | copy-start | bytes 1572868

commit v7 on v6

--- a/solution.py
+++ b/solution.py
@@ -20,7 +20,7 @@
 SAME_TR = ("zh", "y", "x")
 SLOTS = 64
 NAUX = 2048
-BLOCK = 8
+BLOCK = 16
 STEPS = SLOTS // BLOCK
 PARTS = 4
 UNTIL_DIRECT = 2 * 10**10
@@ -64,7 +64,7 @@
 
 
 def both_halves(rows):
-    return jnp.concatenate([rows[:, :CB], rows[:, CB:]], axis=0)
+    return jnp.concatenate([rows[:, :CB], rows[:, CB : 2 * CB]], axis=0)
 
 
 def first_kernel(
@@ -110,13 +110,12 @@
 
     row = lax.broadcasted_iota(jnp.int32, (HALF * V, 1), 0)
     if first:
-        for a in range(AUX):
-            for t in range(TR):
-                slab = arrived_ref[place(a, t), :, : 2 * CB].astype(F32)
-                rows_ref[t, 16 * a : 16 * a + 16] = both_halves(slab).astype(BF16)
         chosen = lax.broadcasted_iota(jnp.int32, (HALF * V, K * V), 1)
         wanted = K * (row % V) + HALF * core + row // V
-        wide = rows_ref[tr]
+        stride = place(0, 1) - place(0, 0)
+        wide = [arrived_ref[place(a, 0) + stride * tr, :, : 2 * CB].astype(F32) for a in range(AUX)]
+        wide = jnp.concatenate([both_halves(slab) for slab in wide], axis=0).astype(BF16)
+        projection = jnp.zeros((K, 128), F32)
     else:
         chosen = lax.broadcasted_iota(jnp.int32, (HALF * V, HALF * V), 1)
         wanted = HALF * AUX * (row % 2) + HALF * (row % V // 2) + row // V
@@ -137,11 +136,17 @@
                 blended_ref[step % 2, V * k : V * k + V, CB * p : CB * p + CB] = piece[V * p : V * p + V]
 
     blend(0)
+    devices = [(a, t) for a in range(AUX) for t in range(TR)]
     for step in range(STEPS):
         rows = slice(step * BLOCK * CB, (step + 1) * BLOCK * CB)
         product = dot(blended_ref[step % 2], virt_ref[rows])
         if step + 1 < STEPS:
             blend(step + 1)
+        if first:
+            for a, t in devices[step::STEPS]:
+                slab = arrived_ref[place(a, t)].astype(F32)
+                rows_ref[t, 16 * a : 16 * a + 16] = both_halves(slab).astype(BF16)
+                projection += slab[:, 2 * CB :]
         if step == 0:
             total_ref[...] = product
         else:
@@ -175,9 +180,6 @@
             high = column.astype(BF16).astype(F32)
             kept = jnp.where(lanes % 32 == j, high, kept)
             kept = jnp.where(lanes % 32 == HALF + j, column - high, kept)
-        projection = jnp.zeros((K, 128), F32)
-        for device in range(PAIRS):
-            projection += arrived_ref[device, :, 2 * CB :].astype(F32)
         extra = jnp.where(lanes // 32 == quarter, projection, kept)
         near = lax.rem(lanes // 32 - quarter + 4, 4) < 2
         extra = jnp.where(near, extra, pltpu.roll(pltpu.roll(extra, 64, 1), 4, 0))[:HALF]
@@ -297,7 +299,7 @@
         out_specs=VMEM,
         out_shape=out,
         scratch_shapes=scratch,
-        compiler_params=params(12),
+        compiler_params=params(20),
     )(live, arrived, occ, virt, *local)
 
 

time: 94.9 us -> 94.8 us (level)
  no operation moved by 1% of the time
where the time goes in v7:
time: 94.8 us; the launch traced here: 94.5 us
  blocking collectives  74 us (78%)
  Pallas kernels  19.1 us (20%)
  between operations  1.37 us (1%)
    all_to_all x4, blocking collectives, exchange(): return lax.all_to_all(x, axes, split_axis=0, concat_axis=0, tiled=True)  66.5 us
    pallas_call x2, Pallas kernels, direct_call(): pl.pallas_call(functools.partial(direct_kernel, first), in_specs=[SMEM] +...  14.6 us
    all_gather x1, blocking collectives, body(): both = lax.all_gather(mine, 'grp')  7.55 us
    pallas_call x1, Pallas kernels, body(): pl.pallas_call(first_kernel, in_specs=[SMEM] + [HBM] * 4, out_specs=[VMEM...  1.95 us

profile of v7, /device:TPU:1, one launch (start us, length us, event | category | flops | bytes accessed | tf_op | source)
XLA Modules:
  0.0 94.5 jit_solution(369912862287835895)
XLA Ops:
  1.3 0.0 slice-start
  1.3 0.0 slice-start.1
  1.3 0.0 slice-start.2
  1.3 0.0 slice-start.3
  1.3 0.0 copy-start
  1.3 1.9 %shard_map.86 = (bf16[64,8,640]{2,1,0:T(8,128)(2,1)S(1)}, f32[2,8,256]{2,1,0:T(8,128)S(1)}, f32[8,256]{1,0:T(8,128)S(1)}, bf16[512,2048]{1,0:T(8,128)(2,1)S(1)}) custom-call(s32[1]{0:T(128)S(6)} %copy.9.live_ref.refs_0_, f32[2,8,256]{2,1,0:T(8,128)} %trial_hbm.1, bf16[512,2048]{1,0:T(8,128)(2,1)} %bitcast.9, f32[1,256]{1,0:T(1,128)} %bitcast.10, f32[2]{0:T(128)} %val_hbm.1), custom_call_target="tpu_custom_call" | custom-call | flops 20000000000 | bytes 2097152 | tf_op jit(solution)/shard_map/pallas_call | solution.py:314
  3.3 25.6 %all_to_all.20.refs_1_ = bf16[64,8,640]{2,1,0:T(8,128)(2,1)S(1)} all-to-all(bf16[64,8,640]{2,1,0:T(8,128)(2,1)S(1)} %get-tuple-element.9), channel_id=1, replica_groups=mesh['grp'=2,'y'=4,'zh'=2,'x'=4,'tr'=2] {'zh','tr','y','x'}, dimensions={0} | all-to-all | bytes 1310720 | tf_op jit(solution)/shard_map/all_to_all | solution.py:312
  28.9 0.0 slice-done
  28.9 0.0 slice-done.1
  28.9 0.0 slice-done.2
  28.9 0.0 slice-done.3
  28.9 0.0 copy-done
  28.9 7.5 %shard_map.87 = bf16[64,4,640]{2,1,0:T(4,128)(2,1)S(1)} custom-call(s32[1]{0:T(128)S(6)} %copy.9.live_ref.refs_0_, bf16[64,8,640]{2,1,0:T(8,128)(2,1)S(1)} %all_to_all.20.refs_1_, bf16[64,64,64]{2,1,0:T(8,128)(2,1)S(1)} %copy-done, bf16[16384,512]{1,0:T(8,128)(2,1)S(1)} %bitcast.6, f32[2,8,256]{2,1,0:T(8,128)S(1)} %get-tuple-element.10.refs_4_.trial_ref, ...), custom_call_target="tpu_custom_call" | custom-call | tf_op jit(solution)/shard_map/pallas_call | solution.py:296
  36.4 14.1 %all_to_all.21.arrived_ref = bf16[64,4,640]{2,1,0:T(4,128)(2,1)S(1)} all-to-all(bf16[64,4,640]{2,1,0:T(4,128)(2,1)S(1)} %shard_map.87), channel_id=1, replica_groups=mesh['grp'=2,'y'=4,'zh'=2,'x'=4,'tr'=2] {'zh','tr','y','x'}, dimensions={0} | all-to-all | bytes 655360 | tf_op jit(solution)/shard_map/all_to_all | solution.py:312
  50.5 1.2 %shard_map.88 = (bf16[32,4,640]{2,1,0:T(4,128)(2,1)S(1)}, f32[8,256]{1,0:T(8,128)S(1)}, f32[8,128]{1,0:T(8,128)S(1)}) custom-call(bf16[64,4,640]{2,1,0:T(4,128)(2,1)S(1)} %all_to_all.21.arrived_ref, bf16[512,2048]{1,0:T(8,128)(2,1)S(1)} %get-tuple-element.12.pair_ref, f32[2,8,256]{2,1,0:T(8,128)S(1)} %get-tuple-element.10.refs_4_.trial_ref, ...), custom_call_target="tpu_custom_call" | custom-call | tf_op jit(solution)/shard_map/pallas_call | solution.py:335
  51.7 12.9 %all_to_all.22.refs_1_ = bf16[32,4,640]{2,1,0:T(4,128)(2,1)S(1)} all-to-all(bf16[32,4,640]{2,1,0:T(4,128)(2,1)S(1)} %get-tuple-element.13), channel_id=1, replica_groups=mesh['grp'=2,'y'=4,'zh'=2,'x'=4,'tr'=2] {'zh','y','x'}, dimensions={0} | all-to-all | bytes 327680 | tf_op jit(solution)/shard_map/all_to_all | solution.py:312
  64.6 7.1 %shard_map.89 = bf16[64,4,640]{2,1,0:T(4,128)(2,1)S(1)} custom-call(s32[1]{0:T(128)S(6)} %copy.9.live_ref.refs_0_, bf16[32,4,640]{2,1,0:T(4,128)(2,1)S(1)} %all_to_all.22.refs_1_, bf16[64,64,64]{2,1,0:T(8,128)(2,1)S(1)} %copy-done, bf16[16384,512]{1,0:T(8,128)(2,1)S(1)} %bitcast.7), custom_call_target="tpu_custom_call" | custom-call | tf_op jit(solution)/shard_map/pallas_call | solution.py:296
  71.7 13.9 %all_to_all.23.arrived_ref = bf16[64,4,640]{2,1,0:T(4,128)(2,1)S(1)} all-to-all(bf16[64,4,640]{2,1,0:T(4,128)(2,1)S(1)} %shard_map.89), channel_id=1, replica_groups=mesh['grp'=2,'y'=4,'zh'=2,'x'=4,'tr'=2] {'zh','tr','y','x'}, dimensions={0} | all-to-all | bytes 655360 | tf_op jit(solution)/shard_map/all_to_all | solution.py:312
  85.6 0.7 shard_map.90
  86.3 7.5 %all-gather = f32[16,384]{1,0:T(8,128)S(1)} all-gather(f32[8,384]{1,0:T(8,128)S(1)} %shard_map.90), channel_id=2, replica_groups=mesh['grp'=2,'y'=4,'zh'=2,'x'=4,'tr'=2] {'grp'}, dimensions={0}, use_global_device_ids=true | all-gather | bytes 36864 | tf_op jit(solution)/shard_map/all_gather | solution.py:356
  93.8 0.7 shard_map.91
  (1 shorter events, 0.0 us)
Async XLA Ops:
  1.3 27.6 %slice-start = ((s8[16777216]{0:T(1024)(128)(4,1)}), s8[4194304]{0:T(1024)(128)(4,1)S(1)}, s32[]{:S(2)}) async-start(s8[16777216]{0:T(1024)(128)(4,1)} %bitcast.4), calls=%async_computation.4 | async-start | bytes 8388608
  1.3 27.6 %slice-start.1 = ((s8[16777216]{0:T(1024)(128)(4,1)}), s8[4194304]{0:T(1024)(128)(4,1)S(1)}, s32[]{:S(2)}) async-start(s8[16777216]{0:T(1024)(128)(4,1)} %bitcast.4), calls=%async_computation.5 | async-start | bytes 8388608
  1.3 27.6 %slice-start.2 = ((s8[16777216]{0:T(1024)(128)(4,1)}), s8[4194304]{0:T(1024)(128)(4,1)S(1)}, s32[]{:S(2)}) async-start(s8[16777216]{0:T(1024)(128)(4,1)} %bitcast.4), calls=%async_computation.6 | async-start | bytes 8388608
  1.3 27.6 %slice-start.3 = ((s8[16777216]{0:T(1024)(128)(4,1)}), s8[4194304]{0:T(1024)(128)(4,1)S(1)}, s32[]{:S(2)}) async-start(s8[16777216]{0:T(1024)(128)(4,1)} %bitcast.4), calls=%async_computation.7 | async-start | bytes 8388608
  1.3 27.6 %copy-start = (bf16[64,64,64]{2,1,0:T(8,128)(2,1)S(1)}, bf16[64,64,64]{2,1,0:T(8,128)(2,1)}, u32[]{:S(2)}) copy-start(bf16[64,64,64]{2,1,0:T(8,128)(2,1)} %refs_2_.3) | copy-start | bytes 1572868

commit v8 on v7

--- a/solution.py
+++ b/solution.py
@@ -63,8 +63,9 @@
     return jnp.where(core == 0, rows[:HALF], rows[HALF:])
 
 
-def both_halves(rows):
-    return jnp.concatenate([rows[:, :CB], rows[:, CB : 2 * CB]], axis=0)
+def both_halves(slab):
+    parts = [slab[:, CB * i : CB * i + CB] for i in (0, 2, 1, 3)]
+    return jnp.concatenate(parts, axis=0)
 
 
 def first_kernel(
@@ -82,8 +83,10 @@
         copy.start()
     copies[0].wait()
     wide = jnp.concatenate([trial_ref[v].astype(BF16) for v in range(2)], axis=1)
+    few = wide.astype(F32)
+    few = jnp.concatenate([few[:HALF], few[HALF:]], axis=1).astype(BF16)
     for device in range(PAIRS):
-        out_ref[device, :, : 2 * CB] = wide
+        out_ref[device, :, : 4 * CB] = few
     copies[1].wait()
     copies[2].wait()
     for v in range(2):
@@ -93,10 +96,13 @@
         copies[3 + i].wait()
         rows = slice(2 * CB // PARTS * i, 2 * CB // PARTS * (i + 1))
         projection += dot(wide[:, rows], pair_ref[rows])
-    projection = projection.astype(BF16)
-    for device in range(PAIRS):
-        tile = device // 4
-        out_ref[device, :, 2 * CB :] = projection[:, 128 * tile : 128 * tile + 128]
+    lanes = lane_ids((HALF, 128))
+    for tile in range(TILES):
+        part = projection[:, 128 * tile : 128 * tile + 128]
+        low, high = part[:HALF], pltpu.roll(part, 64, 1)[HALF:]
+        for quarter in range(4):
+            both = jnp.where(lanes // 32 == quarter, low, high)
+            out_ref[4 * tile + quarter, :, 4 * CB :] = both.astype(BF16)
 
 
 def direct_kernel(first, *refs):
@@ -113,9 +119,9 @@
         chosen = lax.broadcasted_iota(jnp.int32, (HALF * V, K * V), 1)
         wanted = K * (row % V) + HALF * core + row // V
         stride = place(0, 1) - place(0, 0)
-        wide = [arrived_ref[place(a, 0) + stride * tr, :, : 2 * CB].astype(F32) for a in range(AUX)]
+        wide = [arrived_ref[place(a, 0) + stride * tr].astype(F32) for a in range(AUX)]
         wide = jnp.concatenate([both_halves(slab) for slab in wide], axis=0).astype(BF16)
-        projection = jnp.zeros((K, 128), F32)
+        projection = jnp.zeros((HALF, 128), F32)
     else:
         chosen = lax.broadcasted_iota(jnp.int32, (HALF * V, HALF * V), 1)
         wanted = HALF * AUX * (row % 2) + HALF * (row % V // 2) + row // V
@@ -146,7 +152,7 @@
             for a, t in devices[step::STEPS]:
                 slab = arrived_ref[place(a, t)].astype(F32)
                 rows_ref[t, 16 * a : 16 * a + 16] = both_halves(slab).astype(BF16)
-                projection += slab[:, 2 * CB :]
+                projection += slab[:, 4 * CB :]
         if step == 0:
             total_ref[...] = product
         else:
@@ -180,9 +186,9 @@
             high = column.astype(BF16).astype(F32)
             kept = jnp.where(lanes % 32 == j, high, kept)
             kept = jnp.where(lanes % 32 == HALF + j, column - high, kept)
-        extra = jnp.where(lanes // 32 == quarter, projection, kept)
-        near = lax.rem(lanes // 32 - quarter + 4, 4) < 2
-        extra = jnp.where(near, extra, pltpu.roll(pltpu.roll(extra, 64, 1), 4, 0))[:HALF]
+        ahead = lax.rem(lanes // 32 - quarter + 4, 4)
+        kept = jnp.where(ahead < 2, kept, pltpu.roll(kept, 4, 0))[:HALF]
+        extra = jnp.where(ahead[:HALF] % 2 == 0, projection, kept)
     else:
         extra = jnp.zeros((HALF, 128), F32)
         for slab in slabs:
@@ -316,7 +322,7 @@
         in_specs=[SMEM] + [HBM] * 4,
         out_specs=[VMEM] * 4,
         out_shape=[
-            jax.ShapeDtypeStruct((PAIRS, K, 2 * CB + 128), BF16),
+            jax.ShapeDtypeStruct((PAIRS, HALF, 4 * CB + 128), BF16),
             jax.ShapeDtypeStruct((2, K, CB), F32),
             jax.ShapeDtypeStruct((2 * HALF, CB), F32),
             jax.typeof(pair),

time: 94.8 us -> 94.1 us (level)
  no operation moved by 1% of the time
where the time goes in v8:
time: 94.1 us; the launch traced here: 93.8 us
  blocking collectives  73.4 us (78%)
  Pallas kernels  19.1 us (20%)
  between operations  1.37 us (1%)
    all_to_all x4, blocking collectives, exchange(): return lax.all_to_all(x, axes, split_axis=0, concat_axis=0, tiled=True)  65.8 us
    pallas_call x2, Pallas kernels, direct_call(): pl.pallas_call(functools.partial(direct_kernel, first), in_specs=[SMEM] +...  14.5 us
    all_gather x1, blocking collectives, body(): both = lax.all_gather(mine, 'grp')  7.6 us
    pallas_call x1, Pallas kernels, body(): pl.pallas_call(first_kernel, in_specs=[SMEM] + [HBM] * 4, out_specs=[VMEM...  2.02 us

profile of v8, /device:TPU:1, one launch (start us, length us, event | category | flops | bytes accessed | tf_op | source)
XLA Modules:
  0.0 93.8 jit_solution(2746402819162332134)
XLA Ops:
  1.3 0.0 slice-start
  1.3 0.0 slice-start.1
  1.3 0.0 slice-start.2
  1.3 0.0 slice-start.3
  1.3 0.0 copy-start
  1.3 2.0 %shard_map.86 = (bf16[64,4,1152]{2,1,0:T(4,128)(2,1)S(1)}, f32[2,8,256]{2,1,0:T(8,128)S(1)}, f32[8,256]{1,0:T(8,128)S(1)}, bf16[512,2048]{1,0:T(8,128)(2,1)S(1)}) custom-call(s32[1]{0:T(128)S(6)} %copy.9.live_ref.refs_0_, f32[2,8,256]{2,1,0:T(8,128)} %trial_hbm.1, bf16[512,2048]{1,0:T(8,128)(2,1)} %bitcast.9, f32[1,256]{1,0:T(1,128)} %bitcast.10, f32[2]{0:T(128)} %val_hbm.1), custom_call_target="tpu_custom_call" | custom-call | flops 20000000000 | bytes 2097152 | tf_op jit(solution)/shard_map/pallas_call | solution.py:320
  3.4 24.9 %all_to_all.20.refs_1_ = bf16[64,4,1152]{2,1,0:T(4,128)(2,1)S(1)} all-to-all(bf16[64,4,1152]{2,1,0:T(4,128)(2,1)S(1)} %get-tuple-element.9), channel_id=1, replica_groups=mesh['grp'=2,'y'=4,'zh'=2,'x'=4,'tr'=2] {'zh','tr','y','x'}, dimensions={0} | all-to-all | bytes 1179648 | tf_op jit(solution)/shard_map/all_to_all | solution.py:318
  28.2 0.0 slice-done
  28.2 0.0 slice-done.1
  28.2 0.0 slice-done.2
  28.2 0.0 slice-done.3
  28.2 0.0 copy-done
  28.3 7.5 %shard_map.87 = bf16[64,4,640]{2,1,0:T(4,128)(2,1)S(1)} custom-call(s32[1]{0:T(128)S(6)} %copy.9.live_ref.refs_0_, bf16[64,4,1152]{2,1,0:T(4,128)(2,1)S(1)} %all_to_all.20.refs_1_, bf16[64,64,64]{2,1,0:T(8,128)(2,1)S(1)} %copy-done, bf16[16384,512]{1,0:T(8,128)(2,1)S(1)} %bitcast.6, f32[2,8,256]{2,1,0:T(8,128)S(1)} %get-tuple-element.10.refs_4_.trial_ref, ...), custom_call_target="tpu_custom_call" | custom-call | tf_op jit(solution)/shard_map/pallas_call | solution.py:302
  35.8 14.1 %all_to_all.21.arrived_ref = bf16[64,4,640]{2,1,0:T(4,128)(2,1)S(1)} all-to-all(bf16[64,4,640]{2,1,0:T(4,128)(2,1)S(1)} %shard_map.87), channel_id=1, replica_groups=mesh['grp'=2,'y'=4,'zh'=2,'x'=4,'tr'=2] {'zh','tr','y','x'}, dimensions={0} | all-to-all | bytes 655360 | tf_op jit(solution)/shard_map/all_to_all | solution.py:318
  49.8 1.2 %shard_map.88 = (bf16[32,4,640]{2,1,0:T(4,128)(2,1)S(1)}, f32[8,256]{1,0:T(8,128)S(1)}, f32[8,128]{1,0:T(8,128)S(1)}) custom-call(bf16[64,4,640]{2,1,0:T(4,128)(2,1)S(1)} %all_to_all.21.arrived_ref, bf16[512,2048]{1,0:T(8,128)(2,1)S(1)} %get-tuple-element.12.pair_ref, f32[2,8,256]{2,1,0:T(8,128)S(1)} %get-tuple-element.10.refs_4_.trial_ref, ...), custom_call_target="tpu_custom_call" | custom-call | tf_op jit(solution)/shard_map/pallas_call | solution.py:341
  51.0 12.9 %all_to_all.22.refs_1_ = bf16[32,4,640]{2,1,0:T(4,128)(2,1)S(1)} all-to-all(bf16[32,4,640]{2,1,0:T(4,128)(2,1)S(1)} %get-tuple-element.13), channel_id=1, replica_groups=mesh['grp'=2,'y'=4,'zh'=2,'x'=4,'tr'=2] {'zh','y','x'}, dimensions={0} | all-to-all | bytes 327680 | tf_op jit(solution)/shard_map/all_to_all | solution.py:318
  63.9 7.1 %shard_map.89 = bf16[64,4,640]{2,1,0:T(4,128)(2,1)S(1)} custom-call(s32[1]{0:T(128)S(6)} %copy.9.live_ref.refs_0_, bf16[32,4,640]{2,1,0:T(4,128)(2,1)S(1)} %all_to_all.22.refs_1_, bf16[64,64,64]{2,1,0:T(8,128)(2,1)S(1)} %copy-done, bf16[16384,512]{1,0:T(8,128)(2,1)S(1)} %bitcast.7), custom_call_target="tpu_custom_call" | custom-call | tf_op jit(solution)/shard_map/pallas_call | solution.py:302
  71.0 13.9 %all_to_all.23.arrived_ref = bf16[64,4,640]{2,1,0:T(4,128)(2,1)S(1)} all-to-all(bf16[64,4,640]{2,1,0:T(4,128)(2,1)S(1)} %shard_map.89), channel_id=1, replica_groups=mesh['grp'=2,'y'=4,'zh'=2,'x'=4,'tr'=2] {'zh','tr','y','x'}, dimensions={0} | all-to-all | bytes 655360 | tf_op jit(solution)/shard_map/all_to_all | solution.py:318
  84.9 0.7 shard_map.90
  85.6 7.6 %all-gather = f32[16,384]{1,0:T(8,128)S(1)} all-gather(f32[8,384]{1,0:T(8,128)S(1)} %shard_map.90), channel_id=2, replica_groups=mesh['grp'=2,'y'=4,'zh'=2,'x'=4,'tr'=2] {'grp'}, dimensions={0}, use_global_device_ids=true | all-gather | bytes 36864 | tf_op jit(solution)/shard_map/all_gather | solution.py:362
  93.2 0.7 shard_map.91
  (1 shorter events, 0.0 us)
Async XLA Ops:
  1.3 27.0 %slice-start = ((s8[16777216]{0:T(1024)(128)(4,1)}), s8[4194304]{0:T(1024)(128)(4,1)S(1)}, s32[]{:S(2)}) async-start(s8[16777216]{0:T(1024)(128)(4,1)} %bitcast.4), calls=%async_computation.4 | async-start | bytes 8388608
  1.3 26.9 %slice-start.1 = ((s8[16777216]{0:T(1024)(128)(4,1)}), s8[4194304]{0:T(1024)(128)(4,1)S(1)}, s32[]{:S(2)}) async-start(s8[16777216]{0:T(1024)(128)(4,1)} %bitcast.4), calls=%async_computation.5 | async-start | bytes 8388608
  1.3 26.9 %slice-start.2 = ((s8[16777216]{0:T(1024)(128)(4,1)}), s8[4194304]{0:T(1024)(128)(4,1)S(1)}, s32[]{:S(2)}) async-start(s8[16777216]{0:T(1024)(128)(4,1)} %bitcast.4), calls=%async_computation.6 | async-start | bytes 8388608
  1.3 26.9 %slice-start.3 = ((s8[16777216]{0:T(1024)(128)(4,1)}), s8[4194304]{0:T(1024)(128)(4,1)S(1)}, s32[]{:S(2)}) async-start(s8[16777216]{0:T(1024)(128)(4,1)} %bitcast.4), calls=%async_computation.7 | async-start | bytes 8388608
  1.3 26.9 %copy-start = (bf16[64,64,64]{2,1,0:T(8,128)(2,1)S(1)}, bf16[64,64,64]{2,1,0:T(8,128)(2,1)}, u32[]{:S(2)}) copy-start(bf16[64,64,64]{2,1,0:T(8,128)(2,1)} %refs_2_.3) | copy-start | bytes 1572868

commit v9 on v8

--- a/solution.py
+++ b/solution.py
@@ -135,7 +135,8 @@
 
     def blend(step):
         occ = occ_ref[BLOCK * step : BLOCK * step + BLOCK].reshape(BLOCK * V, V)
-        occ = jnp.where(slot < live - step * BLOCK, occ, jnp.zeros_like(occ))
+        if step > 0:
+            occ = jnp.where(slot < live - step * BLOCK, occ, jnp.zeros_like(occ))
         for k in range(HALF):
             piece = dot(occ, vectors_ref[V * k : V * k + V]).astype(BF16)
             for p in range(BLOCK):

time: 94.1 us -> 94.1 us (level)
  no operation moved by 1% of the time
where the time goes in v9:
time: 94.1 us; the launch traced here: 93.8 us
  blocking collectives  73.4 us (78%)
  Pallas kernels  19.1 us (20%)
  between operations  1.37 us (1%)
    all_to_all x4, blocking collectives, exchange(): return lax.all_to_all(x, axes, split_axis=0, concat_axis=0, tiled=True)  65.8 us
    pallas_call x2, Pallas kernels, direct_call(): pl.pallas_call(functools.partial(direct_kernel, first), in_specs=[SMEM] +...  14.5 us
    all_gather x1, blocking collectives, body(): both = lax.all_gather(mine, 'grp')  7.59 us
    pallas_call x1, Pallas kernels, body(): pl.pallas_call(first_kernel, in_specs=[SMEM] + [HBM] * 4, out_specs=[VMEM...  2.02 us

profile of v9, /device:TPU:1, one launch (start us, length us, event | category | flops | bytes accessed | tf_op | source)
XLA Modules:
  0.0 93.8 jit_solution(3329390098061150976)
XLA Ops:
  1.3 0.0 slice-start
  1.3 0.0 slice-start.1
  1.3 0.0 slice-start.2
  1.3 0.0 slice-start.3
  1.3 0.0 copy-start
  1.3 2.0 %shard_map.86 = (bf16[64,4,1152]{2,1,0:T(4,128)(2,1)S(1)}, f32[2,8,256]{2,1,0:T(8,128)S(1)}, f32[8,256]{1,0:T(8,128)S(1)}, bf16[512,2048]{1,0:T(8,128)(2,1)S(1)}) custom-call(s32[1]{0:T(128)S(6)} %copy.9.live_ref.refs_0_, f32[2,8,256]{2,1,0:T(8,128)} %trial_hbm.1, bf16[512,2048]{1,0:T(8,128)(2,1)} %bitcast.9, f32[1,256]{1,0:T(1,128)} %bitcast.10, f32[2]{0:T(128)} %val_hbm.1), custom_call_target="tpu_custom_call" | custom-call | flops 20000000000 | bytes 2097152 | tf_op jit(solution)/shard_map/pallas_call | solution.py:321
  3.4 24.9 %all_to_all.20.refs_1_ = bf16[64,4,1152]{2,1,0:T(4,128)(2,1)S(1)} all-to-all(bf16[64,4,1152]{2,1,0:T(4,128)(2,1)S(1)} %get-tuple-element.9), channel_id=1, replica_groups=mesh['grp'=2,'y'=4,'zh'=2,'x'=4,'tr'=2] {'zh','tr','y','x'}, dimensions={0} | all-to-all | bytes 1179648 | tf_op jit(solution)/shard_map/all_to_all | solution.py:319
  28.2 0.0 slice-done
  28.2 0.0 slice-done.1
  28.2 0.0 slice-done.2
  28.2 0.0 slice-done.3
  28.2 0.0 copy-done
  28.3 7.5 %shard_map.87 = bf16[64,4,640]{2,1,0:T(4,128)(2,1)S(1)} custom-call(s32[1]{0:T(128)S(6)} %copy.9.live_ref.refs_0_, bf16[64,4,1152]{2,1,0:T(4,128)(2,1)S(1)} %all_to_all.20.refs_1_, bf16[64,64,64]{2,1,0:T(8,128)(2,1)S(1)} %copy-done, bf16[16384,512]{1,0:T(8,128)(2,1)S(1)} %bitcast.6, f32[2,8,256]{2,1,0:T(8,128)S(1)} %get-tuple-element.10.refs_4_.trial_ref, ...), custom_call_target="tpu_custom_call" | custom-call | tf_op jit(solution)/shard_map/pallas_call | solution.py:303
  35.7 14.1 %all_to_all.21.arrived_ref = bf16[64,4,640]{2,1,0:T(4,128)(2,1)S(1)} all-to-all(bf16[64,4,640]{2,1,0:T(4,128)(2,1)S(1)} %shard_map.87), channel_id=1, replica_groups=mesh['grp'=2,'y'=4,'zh'=2,'x'=4,'tr'=2] {'zh','tr','y','x'}, dimensions={0} | all-to-all | bytes 655360 | tf_op jit(solution)/shard_map/all_to_all | solution.py:319
  49.8 1.2 %shard_map.88 = (bf16[32,4,640]{2,1,0:T(4,128)(2,1)S(1)}, f32[8,256]{1,0:T(8,128)S(1)}, f32[8,128]{1,0:T(8,128)S(1)}) custom-call(bf16[64,4,640]{2,1,0:T(4,128)(2,1)S(1)} %all_to_all.21.arrived_ref, bf16[512,2048]{1,0:T(8,128)(2,1)S(1)} %get-tuple-element.12.pair_ref, f32[2,8,256]{2,1,0:T(8,128)S(1)} %get-tuple-element.10.refs_4_.trial_ref, ...), custom_call_target="tpu_custom_call" | custom-call | tf_op jit(solution)/shard_map/pallas_call | solution.py:342
  51.0 12.9 %all_to_all.22.refs_1_ = bf16[32,4,640]{2,1,0:T(4,128)(2,1)S(1)} all-to-all(bf16[32,4,640]{2,1,0:T(4,128)(2,1)S(1)} %get-tuple-element.13), channel_id=1, replica_groups=mesh['grp'=2,'y'=4,'zh'=2,'x'=4,'tr'=2] {'zh','y','x'}, dimensions={0} | all-to-all | bytes 327680 | tf_op jit(solution)/shard_map/all_to_all | solution.py:319
  63.9 7.1 %shard_map.89 = bf16[64,4,640]{2,1,0:T(4,128)(2,1)S(1)} custom-call(s32[1]{0:T(128)S(6)} %copy.9.live_ref.refs_0_, bf16[32,4,640]{2,1,0:T(4,128)(2,1)S(1)} %all_to_all.22.refs_1_, bf16[64,64,64]{2,1,0:T(8,128)(2,1)S(1)} %copy-done, bf16[16384,512]{1,0:T(8,128)(2,1)S(1)} %bitcast.7), custom_call_target="tpu_custom_call" | custom-call | tf_op jit(solution)/shard_map/pallas_call | solution.py:303
  71.0 13.9 %all_to_all.23.arrived_ref = bf16[64,4,640]{2,1,0:T(4,128)(2,1)S(1)} all-to-all(bf16[64,4,640]{2,1,0:T(4,128)(2,1)S(1)} %shard_map.89), channel_id=1, replica_groups=mesh['grp'=2,'y'=4,'zh'=2,'x'=4,'tr'=2] {'zh','tr','y','x'}, dimensions={0} | all-to-all | bytes 655360 | tf_op jit(solution)/shard_map/all_to_all | solution.py:319
  84.9 0.7 shard_map.90
  85.6 7.6 %all-gather = f32[16,384]{1,0:T(8,128)S(1)} all-gather(f32[8,384]{1,0:T(8,128)S(1)} %shard_map.90), channel_id=2, replica_groups=mesh['grp'=2,'y'=4,'zh'=2,'x'=4,'tr'=2] {'grp'}, dimensions={0}, use_global_device_ids=true | all-gather | bytes 36864 | tf_op jit(solution)/shard_map/all_gather | solution.py:363
  93.2 0.7 shard_map.91
  (1 shorter events, 0.0 us)
Async XLA Ops:
  1.3 27.0 %slice-start = ((s8[16777216]{0:T(1024)(128)(4,1)}), s8[4194304]{0:T(1024)(128)(4,1)S(1)}, s32[]{:S(2)}) async-start(s8[16777216]{0:T(1024)(128)(4,1)} %bitcast.4), calls=%async_computation.4 | async-start | bytes 8388608
  1.3 26.9 %slice-start.1 = ((s8[16777216]{0:T(1024)(128)(4,1)}), s8[4194304]{0:T(1024)(128)(4,1)S(1)}, s32[]{:S(2)}) async-start(s8[16777216]{0:T(1024)(128)(4,1)} %bitcast.4), calls=%async_computation.5 | async-start | bytes 8388608
  1.3 26.9 %slice-start.2 = ((s8[16777216]{0:T(1024)(128)(4,1)}), s8[4194304]{0:T(1024)(128)(4,1)S(1)}, s32[]{:S(2)}) async-start(s8[16777216]{0:T(1024)(128)(4,1)} %bitcast.4), calls=%async_computation.6 | async-start | bytes 8388608
  1.3 26.9 %slice-start.3 = ((s8[16777216]{0:T(1024)(128)(4,1)}), s8[4194304]{0:T(1024)(128)(4,1)S(1)}, s32[]{:S(2)}) async-start(s8[16777216]{0:T(1024)(128)(4,1)} %bitcast.4), calls=%async_computation.7 | async-start | bytes 8388608
  1.3 26.9 %copy-start = (bf16[64,64,64]{2,1,0:T(8,128)(2,1)S(1)}, bf16[64,64,64]{2,1,0:T(8,128)(2,1)}, u32[]{:S(2)}) copy-start(bf16[64,64,64]{2,1,0:T(8,128)(2,1)} %refs_2_.3) | copy-start | bytes 1572868
